TPU v7x, 32 devices: a whole 2x2x4 slice. The times are simulated.
32 devices in a mesh: grp: 4 (over y, x), pen: 8 (over z, core).
Axes of the slice: x: 2, y: 2, z: 4, core: 2. Of those that a mesh axis runs over, the one named last changes fastest.
Arguments:
- columns: float32 [2, 512, 512, 512], P(None, 'grp', 'pen'), may hold values from -6 to 6
- basis_in_x: float32 [512, 512], replicated, may hold values from -0.25 to 0.25
- basis_in_y: float32 [512, 512], replicated, may hold values from -0.25 to 0.25
- basis_in_z: float32 [512, 512], replicated, may hold values from -0.25 to 0.25
- basis_out_x: float32 [512, 512], replicated, may hold values from -0.25 to 0.25
- basis_out_y: float32 [512, 512], replicated, may hold values from -0.25 to 0.25
- basis_out_z: float32 [512, 512], replicated, may hold values from -0.25 to 0.25
- eig_x: float32 [512], replicated, may hold values from 0.05 to 3
- eig_y: float32 [512], replicated, may hold values from 0.05 to 3
- eig_z: float32 [512], replicated, may hold values from 0.05 to 3
- shift_table: float32 [64], replicated, may hold values from 0.5 to 8
- shift_index: int32 [2], replicated, may hold values from 0 to 63
Outputs:
- solved: float32 [2, 512, 512, 512], P(None, 'grp', 'pen')
Inputs may be any that keep to these rules, and one draw needn't show every extreme that they name: `shift_index`: indices into shift_table.
All inputs are finite; a program needn't handle non-finite values.
Results may differ from a plain program's by a relative error of at most 0.00007.
Values sent between devices are 32-bit elements; how exact they have to be, the bound alone decides.
No kernel may reach another device: no remote copies, remote signals or barrier semaphores. Data moves between devices by JAX's collectives and lax.ppermute only.
A program may use at most 256 MiB of HBM per device.

v0:
```python
import jax
import jax.numpy as jnp
from jax import lax
from jax.sharding import PartitionSpec as P


def solve_slab(
    volume,
    basis_in_x,
    basis_in_y,
    basis_in_z,
    basis_out_x,
    basis_out_y,
    basis_out_z,
    eig_x,
    eig_y,
    eig_z,
    shift_value,
):
    highest = lax.Precision.HIGHEST
    count, x_local, y_local, length = volume.shape
    pen_count = lax.axis_size("pen")
    grp_count = lax.axis_size("grp")
    z_slab = length // (pen_count * grp_count)
    forward = jnp.einsum("kz,cxyz->ckxy", basis_in_z, volume, precision=highest)
    planes = lax.all_to_all(
        lax.all_to_all(forward, "grp", split_axis=1, concat_axis=2, tiled=True),
        "pen",
        split_axis=1,
        concat_axis=3,
        tiled=True,
    )
    spectral = jnp.einsum("ix,ckxy->ckiy", basis_in_x, planes, precision=highest)
    spectral = jnp.einsum("jy,ckiy->ckij", basis_in_y, spectral, precision=highest)
    start_row = (lax.axis_index("grp") * pen_count + lax.axis_index("pen")) * z_slab
    eig_z_part = lax.dynamic_slice_in_dim(eig_z, start_row, z_slab)
    shift_wide = shift_value[:, None, None, None]
    denominator = (
        eig_z_part[None, :, None, None]
        + eig_x[None, None, :, None]
        + eig_y[None, None, None, :]
        + shift_wide
    )
    scaled = jnp.sqrt(2.0 * shift_wide) * spectral / denominator
    back = jnp.einsum("xi,ckij->ckxj", basis_out_x, scaled, precision=highest)
    back = jnp.einsum("yj,ckxj->ckxy", basis_out_y, back, precision=highest)
    returned = lax.all_to_all(
        lax.all_to_all(back, "grp", split_axis=2, concat_axis=1, tiled=True),
        "pen",
        split_axis=3,
        concat_axis=1,
        tiled=True,
    )
    returned = returned.reshape(count, pen_count, grp_count, z_slab, x_local, y_local)
    table = basis_out_z.reshape(length, grp_count, pen_count, z_slab)
    return jnp.einsum("zgpk,cpgkxy->cxyz", table, returned, precision=highest)


def per_device(
    columns,
    basis_in_x,
    basis_in_y,
    basis_in_z,
    basis_out_x,
    basis_out_y,
    basis_out_z,
    eig_x,
    eig_y,
    eig_z,
    shift_table,
    shift_index,
):
    shift_values = shift_table[shift_index]
    operands = (
        basis_in_x,
        basis_in_y,
        basis_in_z,
        basis_out_x,
        basis_out_y,
        basis_out_z,
        eig_x,
        eig_y,
        eig_z,
    )

    def solve_some(volume, shifts):
        return solve_slab(volume, *operands, shifts)

    pieces = [
        solve_some(columns[column : column + 1], shift_values[column : column + 1])
        for column in range(columns.shape[0])
    ]
    return jnp.concatenate(pieces, axis=0)


def solution(mesh):
    in_specs = (P(None, "grp", "pen", None), P(), P(), P(), P(), P(), P(), P(), P(), P(), P(), P())
    out_specs = P(None, "grp", "pen", None)
    return jax.shard_map(
        per_device, mesh=mesh, in_specs=in_specs, out_specs=out_specs, check_vma=False
    )
```

profile of v0, /device:TPU:0, one launch (start us, length us, event | category | flops | bytes accessed | tf_op | source)
XLA Modules:
  0.0 2450.9 jit_solution(14090228158960818563)
XLA Ops:
  17.2 35.1 %fusion.34 = f32[1,512,128,64]{1,2,3,0:T(8,128)} fusion(f32[1,128,64,512]{3,2,1,0:T(8,128)S(1)} %get-tuple-element.5, f32[512,512]{1,0:T(8,128)S(1)} %copy-done), kind=kOutput, calls=%fused_computation.30 | convolution fusion | flops 25769803776 | bytes 34603008 | tf_op jit(solution)/shard_map/kz,cxyz->ckxy/dot_general | solution.py:25
  76.1 41.0 %fusion.35 = f32[1,512,128,64]{1,2,3,0:T(8,128)} fusion(f32[1,128,64,512]{3,2,1,0:T(8,128)} %get-tuple-element.6, f32[512,512]{1,0:T(8,128)S(1)} %copy-done), kind=kOutput, calls=%fused_computation.31 | convolution fusion | flops 25769803776 | bytes 34603008 | tf_op jit(solution)/shard_map/kz,cxyz->ckxy/dot_general | solution.py:25
  133.5 126.3 %all-to-all-done = f32[1,512,128,64]{2,3,0,1:T(8,128)} async-done(((f32[1,512,128,64]{2,3,0,1:T(8,128)}), f32[1,512,128,64]{2,3,0,1:T(8,128)}, u32[]{:S(2)}, u32[]{:S(2)}) %all-to-all-start) | async-done | bytes 16777248 | tf_op jit(solution)/shard_map/all_to_all | solution.py:27
  283.5 17.5 copy.105
  301.0 147.8 %all-to-all-done.4 = f32[1,512,128,64]{2,3,0,1:T(8,128)} async-done(((f32[1,512,128,64]{2,3,0,1:T(8,128)}), f32[1,512,128,64]{2,3,0,1:T(8,128)}, u32[]{:S(2)}, u32[]{:S(2)}) %all-to-all-start.4) | async-done | bytes 16777248 | tf_op jit(solution)/shard_map/all_to_all | solution.py:27
  471.5 17.5 copy.121
  489.0 329.6 %all-to-all-done.1 = f32[1,128,512,64]{2,3,0,1:T(8,128)} async-done(((f32[1,128,512,64]{2,3,0,1:T(8,128)}), f32[1,128,512,64]{2,3,0,1:T(8,128)}, u32[]{:S(2)}, u32[]{:S(2)}) %all-to-all-start.1) | async-done | bytes 16777248 | tf_op jit(solution)/shard_map/all_to_all | solution.py:26
  839.5 32.1 %fusion.52 = f32[16,512,512]{2,1,0:T(8,128)S(1)} fusion(f32[16,512,512]{1,2,0:T(8,128)} %bitcast.138, f32[512,512]{1,0:T(8,128)S(1)} %copy-done.3), kind=kOutput, calls=%fused_computation.48 | convolution fusion | flops 25769803776 | bytes 34603008 | tf_op jit(solution)/shard_map/ix,ckxy->ckiy/dot_general | solution.py:33
  871.6 58.0 %fusion.18 = f32[16,512,512]{2,1,0:T(8,128)} fusion(f32[16,512,512]{2,1,0:T(8,128)S(1)} %fusion.52, f32[512,512]{1,0:T(8,128)S(1)} %copy-done.4), kind=kOutput, calls=%fused_computation.22 | convolution fusion | flops 25769803776 | bytes 34603008 | tf_op jit(solution)/shard_map/jy,ckiy->ckij/dot_general | solution.py:34
  929.6 63.6 %fusion.1 = f32[16,512,512]{2,1,0:T(8,128)} fusion(f32[16,512,512]{2,1,0:T(8,128)} %fusion.18, f32[]{:T(128)} %bitcast.16, f32[512]{0:T(512)S(1)} %copy-done.10, f32[16,512]{1,0:T(8,128)S(1)} %broadcast_add_fusion, f32[]{:T(128)} %bitcast, f32[512,512]{1,0:T(8,128)S(1)} %copy-done.8), kind=kOutput, calls=%fused_computation.5 | convolution fusion | flops 25786580992 | bytes 34637832 | tf_op jit(solution)/shard_map/xi,ckij->ckxj/dot_general | solution.py:45
  993.2 57.7 %fusion.22 = f32[1,16,512,512]{3,2,1,0:T(8,128)S(1)} fusion(f32[16,512,512]{2,1,0:T(8,128)} %fusion.1, f32[512,512]{1,0:T(8,128)S(1)} %copy-done.5), kind=kOutput, calls=%fused_computation.26 | convolution fusion | flops 25769803776 | bytes 34603008 | tf_op jit(solution)/shard_map/yj,ckxj->ckxy/dot_general | solution.py:46
  1051.0 21.0 copy.110
  1071.9 116.0 %all-to-all-done.5 = f32[1,128,512,64]{2,3,0,1:T(8,128)} async-done(((f32[1,128,512,64]{2,3,0,1:T(8,128)}), f32[1,128,512,64]{2,3,0,1:T(8,128)}, u32[]{:S(2)}, u32[]{:S(2)}) %all-to-all-start.5) | async-done | bytes 16777248 | tf_op jit(solution)/shard_map/all_to_all | solution.py:26
  1207.9 32.0 %fusion.50 = f32[16,512,512]{2,1,0:T(8,128)S(1)} fusion(f32[16,512,512]{1,2,0:T(8,128)} %bitcast.139, f32[512,512]{1,0:T(8,128)S(1)} %copy-done.3), kind=kOutput, calls=%fused_computation.46 | convolution fusion | flops 25769803776 | bytes 34603008 | tf_op jit(solution)/shard_map/ix,ckxy->ckiy/dot_general | solution.py:33
  1240.0 58.0 %fusion.12 = f32[16,512,512]{2,1,0:T(8,128)} fusion(f32[16,512,512]{2,1,0:T(8,128)S(1)} %fusion.50, f32[512,512]{1,0:T(8,128)S(1)} %copy-done.4), kind=kOutput, calls=%fused_computation.16 | convolution fusion | flops 25769803776 | bytes 34603008 | tf_op jit(solution)/shard_map/jy,ckiy->ckij/dot_general | solution.py:34
  1297.9 63.2 %fusion.4 = f32[16,512,512]{2,1,0:T(8,128)} fusion(f32[16,512,512]{2,1,0:T(8,128)} %fusion.12, f32[]{:T(128)} %bitcast.47, f32[]{:T(128)} %bitcast.34, f32[512]{0:T(512)S(1)} %copy-done.10, f32[16,512]{1,0:T(8,128)S(1)} %broadcast_add_fusion, f32[512,512]{1,0:T(8,128)S(1)} %copy-done.9), kind=kOutput, calls=%fused_computation.7 | convolution fusion | flops 25786580992 | bytes 34637832 | tf_op jit(solution)/shard_map/xi,ckij->ckxj/dot_general | solution.py:45
  1361.2 57.5 %fusion.28 = f32[1,16,512,512]{3,2,1,0:T(8,128)S(1)} fusion(f32[16,512,512]{2,1,0:T(8,128)} %fusion.4, f32[512,512]{1,0:T(8,128)S(1)} %copy-done.5), kind=kOutput, calls=%fused_computation.28 | convolution fusion | flops 25769803776 | bytes 34603008 | tf_op jit(solution)/shard_map/yj,ckxj->ckxy/dot_general | solution.py:46
  1418.7 21.0 copy.126
  1485.9 143.3 %all-to-all-done.6 = f32[1,16,512,512]{3,1,0,2:T(8,128)} async-done(((f32[1,16,512,512]{3,1,0,2:T(8,128)}), f32[1,16,512,512]{3,1,0,2:T(8,128)}, u32[]{:S(2)}, u32[]{:S(2)}) %all-to-all-start.6) | async-done | bytes 16777248 | tf_op jit(solution)/shard_map/all_to_all | solution.py:48
  1674.4 324.5 %all-to-all-done.3 = f32[1,64,128,512]{2,1,0,3:T(8,128)} async-done(((f32[1,64,128,512]{2,1,0,3:T(8,128)}), f32[1,64,128,512]{2,1,0,3:T(8,128)}, u32[]{:S(2)}, u32[]{:S(2)}) %all-to-all-start.3) | async-done | bytes 16777248 | tf_op jit(solution)/shard_map/all_to_all | solution.py:47
  2005.0 31.1 %fusion.25 = f32[1,128,64,512]{3,1,2,0:T(8,128)} fusion(f32[512,4,8,16,1]{0,3,2,1,4:T(8,128)S(1)} %bitcast.146, f32[8,4,16,128,64]{3,2,1,4,0:T(8,128)} %bitcast.72), kind=kOutput, calls=%fused_computation.27 | convolution fusion | flops 25769803776 | bytes 34603008 | tf_op jit(solution)/shard_map/zgpk,cpgkxy->cxyz/dot_general | solution.py:56
  2036.1 332.2 %all-to-all-done.7 = f32[1,64,128,512]{2,1,0,3:T(8,128)} async-done(((f32[1,64,128,512]{2,1,0,3:T(8,128)}), f32[1,64,128,512]{2,1,0,3:T(8,128)}, u32[]{:S(2)}, u32[]{:S(2)}) %all-to-all-start.7) | async-done | bytes 16777248 | tf_op jit(solution)/shard_map/all_to_all | solution.py:47
  2368.3 31.3 %fusion.31 = f32[1,128,64,512]{3,1,2,0:T(8,128)} fusion(f32[512,4,8,16,1]{0,3,2,1,4:T(8,128)S(1)} %bitcast.147, f32[8,4,16,128,64]{3,2,1,4,0:T(8,128)} %bitcast.85), kind=kOutput, calls=%fused_computation.29 | convolution fusion | flops 25769803776 | bytes 34603008 | tf_op jit(solution)/shard_map/zgpk,cpgkxy->cxyz/dot_general | solution.py:56
  2413.3 37.4 %copy.133 = f32[2,128,64,512]{3,2,1,0:T(8,128)} copy(f32[2,128,64,512]{3,1,2,0:T(8,128)S(1)} %pad_maximum_fusion) | data formatting | bytes 67108864 | tf_op jit(solution)/shard_map/concatenate | solution.py:93
  (54 shorter events, 254.2 us)
Async XLA Ops:
  0.0 17.2 copy-start
  68.9 191.0 %all-to-all-start = ((f32[1,512,128,64]{2,3,0,1:T(8,128)}), f32[1,512,128,64]{2,3,0,1:T(8,128)}, u32[]{:S(2)}, u32[]{:S(2)}) async-start(f32[1,512,128,64]{2,3,0,1:T(8,128)} %copy.103), calls=%async_computation | async-start | bytes 33554432 | tf_op jit(solution)/shard_map/all_to_all | solution.py:27
  259.9 188.9 %all-to-all-start.4 = ((f32[1,512,128,64]{2,3,0,1:T(8,128)}), f32[1,512,128,64]{2,3,0,1:T(8,128)}, u32[]{:S(2)}, u32[]{:S(2)}) async-start(f32[1,512,128,64]{2,3,0,1:T(8,128)} %copy.119), calls=%async_computation.4 | async-start | bytes 33554432 | tf_op jit(solution)/shard_map/all_to_all | solution.py:27
  448.8 369.8 %all-to-all-start.1 = ((f32[1,128,512,64]{2,3,0,1:T(8,128)}), f32[1,128,512,64]{2,3,0,1:T(8,128)}, u32[]{:S(2)}, u32[]{:S(2)}) async-start(f32[1,128,512,64]{2,3,0,1:T(8,128)} %copy.105), calls=%async_computation.1 | async-start | bytes 33554432 | tf_op jit(solution)/shard_map/all_to_all | solution.py:26
  489.0 335.3 %copy-start.11 = (s32[2]{0:T(128)S(1)}, s32[2]{0:T(128)}, u32[]{:S(2)}) copy-start(s32[2]{0:T(128)} %param.23) | copy-start | bytes 28
  489.0 335.4 %copy-start.2 = (f32[64]{0:T(128)S(1)}, f32[64]{0:T(128)}, u32[]{:S(2)}) copy-start(f32[64]{0:T(128)} %param.22) | copy-start | bytes 772
  489.0 338.1 %copy-start.7 = (f32[512]{0:T(512)S(1)}, f32[512]{0:T(512)}, u32[]{:S(2)}) copy-start(f32[512]{0:T(512)} %param.19) | copy-start | bytes 6148
  818.6 369.4 %all-to-all-start.5 = ((f32[1,128,512,64]{2,3,0,1:T(8,128)}), f32[1,128,512,64]{2,3,0,1:T(8,128)}, u32[]{:S(2)}, u32[]{:S(2)}) async-start(f32[1,128,512,64]{2,3,0,1:T(8,128)} %copy.121), calls=%async_computation.5 | async-start | bytes 33554432 | tf_op jit(solution)/shard_map/all_to_all | solution.py:26
  827.2 12.3 copy-start.3
  839.5 32.1 %copy-start.4 = (f32[512,512]{1,0:T(8,128)S(1)}, f32[512,512]{1,0:T(8,128)}, u32[]{:S(2)}) copy-start(f32[512,512]{1,0:T(8,128)} %param.14) | copy-start | bytes 3145732
  871.6 58.0 %copy-start.8 = (f32[512,512]{1,0:T(8,128)S(1)}, f32[512,512]{1,0:T(8,128)}, u32[]{:S(2)}) copy-start(f32[512,512]{1,0:T(8,128)} %param.16) | copy-start | bytes 3145732
  871.6 58.0 %copy-start.10 = (f32[512]{0:T(512)S(1)}, f32[512]{0:T(512)}, u32[]{:S(2)}) copy-start(f32[512]{0:T(512)} %param.20) | copy-start | bytes 6148
  929.6 63.6 %copy-start.5 = (f32[512,512]{1,0:T(8,128)S(1)}, f32[512,512]{1,0:T(8,128)}, u32[]{:S(2)}) copy-start(f32[512,512]{1,0:T(8,128)} %param.17) | copy-start | bytes 3145732
  1188.0 251.8 %all-to-all-start.2 = ((f32[1,16,512,512]{3,1,0,2:T(8,128)}), f32[1,16,512,512]{3,1,0,2:T(8,128)}, u32[]{:S(2)}, u32[]{:S(2)}) async-start(f32[1,16,512,512]{3,1,0,2:T(8,128)} %copy.110), calls=%async_computation.2 | async-start | bytes 33554432 | tf_op jit(solution)/shard_map/all_to_all | solution.py:48
  1239.9 58.0 %copy-start.9 = (f32[512,512]{1,0:T(8,128)S(1)}, f32[512,512]{1,0:T(8,128)}, u32[]{:S(2)}) copy-start(f32[512,512]{1,0:T(8,128)} %param.16) | copy-start | bytes 3145732
  1439.8 189.4 %all-to-all-start.6 = ((f32[1,16,512,512]{3,1,0,2:T(8,128)}), f32[1,16,512,512]{3,1,0,2:T(8,128)}, u32[]{:S(2)}, u32[]{:S(2)}) async-start(f32[1,16,512,512]{3,1,0,2:T(8,128)} %copy.126), calls=%async_computation.6 | async-start | bytes 33554432 | tf_op jit(solution)/shard_map/all_to_all | solution.py:48
  1629.2 369.8 %all-to-all-start.3 = ((f32[1,64,128,512]{2,1,0,3:T(8,128)}), f32[1,64,128,512]{2,1,0,3:T(8,128)}, u32[]{:S(2)}, u32[]{:S(2)}) async-start(f32[1,64,128,512]{2,1,0,3:T(8,128)} %copy.113), calls=%async_computation.3 | async-start | bytes 33554432 | tf_op jit(solution)/shard_map/all_to_all | solution.py:47
  1674.4 330.2 %copy-start.6 = (f32[512,512]{1,0:T(8,128)S(1)}, f32[512,512]{1,0:T(8,128)}, u32[]{:S(2)}) copy-start(f32[512,512]{1,0:T(8,128)} %param.18) | copy-start | bytes 3145732
  1999.0 369.4 %all-to-all-start.7 = ((f32[1,64,128,512]{2,1,0,3:T(8,128)}), f32[1,64,128,512]{2,1,0,3:T(8,128)}, u32[]{:S(2)}, u32[]{:S(2)}) async-start(f32[1,64,128,512]{2,1,0,3:T(8,128)} %copy.129), calls=%async_computation.7 | async-start | bytes 33554432 | tf_op jit(solution)/shard_map/all_to_all | solution.py:47
  2413.3 37.4 %copy-start.1 = (f32[512,512]{1,0:T(8,128)S(1)}, f32[512,512]{1,0:T(8,128)}, u32[]{:S(2)}) copy-start(f32[512,512]{1,0:T(8,128)} %param.15) | copy-start | bytes 3145732
where the time goes:
time: 2460 us; the launch traced here: 2450 us
  waiting for transfers between devices  1520 us (62%)
  matrix products  561 us (23%)
  local copies, waits for them, and re-layouts  303 us (12%)
  starting transfers between devices  52 us (2%)
    all_to_all x2, waiting for transfers between devices, solve_slab(): lax.all_to_all(lax.all_to_all(back, 'grp', split_axis=2, concat_axis=1, t...  657 us
    all_to_all x2, waiting for transfers between devices, solve_slab(): lax.all_to_all(lax.all_to_all(forward, 'grp', split_axis=1, concat_axis=2...  446 us
    all_to_all x2, waiting for transfers between devices, solve_slab(): lax.all_to_all(forward, 'grp', split_axis=1, concat_axis=2, tiled=True)  274 us
    all_to_all x2, waiting for transfers between devices, solve_slab(): lax.all_to_all(back, 'grp', split_axis=2, concat_axis=1, tiled=True)  143 us
    dot_general x2, matrix products, solve_slab(): back = jnp.einsum('xi,ckij->ckxj', basis_out_x, scaled, precision=highest)  127 us
    dot_general x2, matrix products, solve_slab(): jnp.einsum('jy,ckiy->ckij', basis_in_y, spectral, precision=highest)  116 us
    dot_general x2, matrix products, solve_slab(): back = jnp.einsum('yj,ckxj->ckxy', basis_out_y, back, precision=highest)  115 us
    all_to_all x6, local copies, waits for them, and re-layouts, solve_slab(): lax.all_to_all(back, 'grp', split_axis=2, concat_axis=1, tiled=True)  78.1 us
  transfers between devices with their start and end apart: 8, of which 7 were waited for; matrix products, arithmetic and copies ran while one was open for 30% of the time, Pallas kernels for 0%

commit v1 on v0

v1 whole, which is shorter than its diff:
```python
import jax
import jax.numpy as jnp
from jax import lax
from jax.experimental import pallas as pl
from jax.experimental.pallas import tpu as pltpu
from jax.sharding import PartitionSpec as P

CHUNKS = 1
LANES = 128
ROWS = 8
VMEM = 56 * 2**20
F32, BF16 = jnp.float32, jnp.bfloat16
BOTH = ("grp", "pen")


def table_parts(table, axis):
    high = lax.reduce_precision(table, exponent_bits=8, mantissa_bits=7)
    low = (table - high).astype(BF16)
    high = high.astype(BF16)
    return jnp.concatenate([high, low, high], axis=axis)


def data_parts(data, axis):
    high = data.astype(BF16)
    low = (data - high.astype(F32)).astype(BF16)
    return jnp.concatenate([high, high, low], axis=axis)


def contract(a, b, dims=((1,), (0,))):
    return lax.dot_general(a, b, (dims, ((), ())), preferred_element_type=F32)


def cost(flops, arrays):
    return pl.CostEstimate(
        flops=flops, bytes_accessed=sum(4 * a.size for a in arrays), transcendentals=0
    )


def params():
    return pltpu.CompilerParams(
        dimension_semantics=("arbitrary",), vmem_limit_bytes=VMEM
    )


def whole(shape):
    return pl.BlockSpec(shape, lambda i: (0,) * len(shape))


def z_in(columns, column, table, members):
    _, x_size, y_size, length = columns.shape
    rows, triple = table.shape
    part, tiles = rows // members, length // LANES
    out = jax.ShapeDtypeStruct((members, part, y_size, x_size), F32)

    def body(*refs):
        flat = [r.at[0].reshape(x_size * ROWS, LANES) for r in refs[:tiles]]
        tab, out = refs[tiles], refs[tiles + 1].reshape(rows * ROWS, x_size)
        for y in range(0, ROWS, 2):
            pair = jnp.concatenate(
                [
                    jnp.concatenate(
                        [f[pl.ds(y + d, x_size, stride=ROWS), :] for f in flat], axis=1
                    )
                    for d in range(2)
                ],
                axis=0,
            )
            done = contract(tab[...], data_parts(pair, 1), ((1,), (1,)))
            for d in range(2):
                out[pl.ds(y + d, rows, stride=ROWS), :] = done[
                    :, d * x_size : (d + 1) * x_size
                ]

    def tile(t):
        return pl.BlockSpec((1, x_size, ROWS, LANES), lambda i: (column, 0, i, t))

    return pl.pallas_call(
        body,
        grid=(y_size // ROWS,),
        in_specs=[tile(t) for t in range(tiles)] + [whole(table.shape)],
        out_specs=pl.BlockSpec((members, part, ROWS, x_size), lambda i: (0, 0, i, 0)),
        out_shape=out,
        compiler_params=params(),
        cost_estimate=cost(2 * rows * triple * x_size * y_size, [columns[0], out]),
    )(*[columns] * tiles, table)


def planes(blocks, groups, tables, eig_x, eig_y, eig_z, shift):
    members, k_size, y_size, x_size = blocks.shape
    slots = members // groups
    length = slots * y_size
    triple = 3 * length

    def body(data, y_in, x_in, x_out, y_out, ex, ey, ez, sh, out):
        plane = jnp.concatenate(
            [
                jnp.concatenate(
                    [data[g * slots + p, 0] for p in range(slots)], axis=0
                )
                for g in range(groups)
            ],
            axis=1,
        )
        spectral = contract(y_in[...], data_parts(plane, 0))
        spectral = contract(data_parts(spectral, 1), x_in[...])
        value = sh[0]
        root = jnp.sqrt(2.0 * jnp.full((1, length), value, F32))
        denominator = (ex[...] + ey[...]) + (ez[pl.program_id(0)] + value)
        scaled = root * spectral / denominator
        back = contract(data_parts(scaled, 1), x_out[...])
        back = contract(y_out[...], data_parts(back, 0))
        for g in range(groups):
            for p in range(slots):
                out[g * slots + p, 0] = back[
                    p * y_size : (p + 1) * y_size, g * x_size : (g + 1) * x_size
                ]

    block = pl.BlockSpec((members, 1, y_size, x_size), lambda i: (0, i, 0, 0))
    smem = pl.BlockSpec(memory_space=pltpu.SMEM)
    return pl.pallas_call(
        body,
        grid=(k_size,),
        in_specs=[block]
        + [whole(t.shape) for t in tables]
        + [whole((1, length)), whole((length, 1)), smem, smem],
        out_specs=block,
        out_shape=jax.ShapeDtypeStruct(blocks.shape, F32),
        compiler_params=params(),
        cost_estimate=cost(8 * triple * length * length * k_size, [blocks, blocks]),
    )(
        blocks,
        *tables,
        eig_x.reshape(1, length),
        eig_y.reshape(length, 1),
        eig_z,
        shift.reshape(1),
    )


def z_out(chunks, table, column, shape, earlier):
    members, part, y_size, x_size = chunks[0].shape
    triple, length = table.shape
    tiles, count, rows = length // LANES, len(chunks), members * part

    def body(*refs):
        flat = [r.reshape(rows * ROWS, x_size) for r in refs[:count]]
        tab, out, turned = refs[count], refs[-2], refs[-1]
        for y in range(0, ROWS, 2):
            pair = jnp.concatenate(
                [
                    jnp.concatenate(
                        [f[pl.ds(y + d, rows, stride=ROWS), :] for f in flat], axis=0
                    )
                    for d in range(2)
                ],
                axis=1,
            )
            done = contract(data_parts(pair.T, 1), tab[...])
            for d in range(2):
                for t in range(tiles):
                    turned[t, pl.ds(y + d, x_size, stride=ROWS), :] = done[
                        d * x_size : (d + 1) * x_size, t * LANES : (t + 1) * LANES
                    ]
        for t in range(tiles):
            out[0, :, :, t * LANES : (t + 1) * LANES] = turned[t].reshape(
                x_size, ROWS, LANES
            )

    given = [] if earlier is None else [earlier]
    return pl.pallas_call(
        body,
        grid=(y_size // ROWS,),
        in_specs=[
            pl.BlockSpec((members, part, ROWS, x_size), lambda i: (0, 0, i, 0))
        ]
        * count
        + [whole(table.shape)]
        + [pl.BlockSpec(memory_space=pl.ANY)] * len(given),
        out_specs=pl.BlockSpec((1, x_size, ROWS, length), lambda i: (column, 0, i, 0)),
        out_shape=jax.ShapeDtypeStruct(shape, F32),
        scratch_shapes=[pltpu.VMEM((tiles, x_size * ROWS, LANES), F32)],
        input_output_aliases={count + 1: 0} if given else {},
        compiler_params=params(),
        cost_estimate=cost(
            2 * triple * length * x_size * y_size, [*chunks, *chunks]
        ),
    )(*chunks, table, *given)


def z_in_plain(columns, column, table, members):
    exact = dict(precision=lax.Precision.HIGHEST)
    done = jnp.einsum("kz,xyz->kyx", table, columns[column], **exact)
    return done.reshape(members, -1, *done.shape[1:])


def planes_plain(blocks, groups, tables, eig_x, eig_y, eig_z, shift):
    exact = dict(precision=lax.Precision.HIGHEST)
    y_in, x_in, x_out, y_out = tables
    members, k_size, y_size, x_size = blocks.shape
    data = blocks.reshape(groups, members // groups, k_size, y_size, x_size)
    plane = data.transpose(2, 1, 3, 0, 4).reshape(
        k_size, members // groups * y_size, groups * x_size
    )
    spectral = jnp.einsum("jy,kyx->kjx", y_in, plane, **exact)
    spectral = jnp.einsum("kjx,xi->kji", spectral, x_in, **exact)
    denominator = eig_x[None, None] + eig_y[None, :, None] + eig_z[:, None, None] + shift
    scaled = jnp.sqrt(2.0 * shift) * spectral / denominator
    back = jnp.einsum("kji,ix->kjx", scaled, x_out, **exact)
    back = jnp.einsum("yj,kjx->kyx", y_out, back, **exact)
    back = back.reshape(k_size, members // groups, y_size, groups, x_size)
    return back.transpose(3, 1, 0, 2, 4).reshape(blocks.shape)


def z_out_plain(chunks, table, column, shape, earlier):
    exact = dict(precision=lax.Precision.HIGHEST)
    rows = jnp.concatenate([c.reshape(-1, *c.shape[2:]) for c in chunks])
    done = jnp.einsum("kyx,kz->xyz", rows, table, **exact)
    result = jnp.zeros(shape, F32) if earlier is None else earlier
    return result.at[column].set(done)


def per_device(
    columns,
    basis_in_x,
    basis_in_y,
    basis_in_z,
    basis_out_x,
    basis_out_y,
    basis_out_z,
    eig_x,
    eig_y,
    eig_z,
    shift_table,
    shift_index,
):
    count, x_size, y_size, length = columns.shape
    slots, groups = lax.axis_size("pen"), lax.axis_size("grp")
    members = slots * groups
    k_size = length // members
    chunks = CHUNKS if k_size % CHUNKS == 0 else 1
    chunk = k_size // chunks
    shift = shift_table[shift_index]
    tiled = x_size % LANES == 0 and y_size % ROWS == 0 and length % LANES == 0
    parts = table_parts if tiled else lambda table, axis: table
    to_z, across, from_z = (
        (z_in, planes, z_out) if tiled else (z_in_plain, planes_plain, z_out_plain)
    )

    rows = basis_in_z.reshape(members, chunks, chunk, length)
    in_tables = [parts(rows[:, m].reshape(-1, length), 1) for m in range(chunks)]
    cols = basis_out_z.T.reshape(members, chunks, chunk, length)
    out_table = parts(cols.transpose(1, 0, 2, 3).reshape(length, length), 0)
    tables = [
        parts(basis_in_y, 1),
        parts(basis_in_x.T, 0),
        parts(basis_out_x.T, 0),
        parts(basis_out_y, 1),
    ]
    first = lax.axis_index(BOTH) * k_size

    def exchange(blocks):
        return lax.all_to_all(blocks, BOTH, split_axis=0, concat_axis=0, tiled=True)

    units = [(c, m) for c in range(count) for m in range(chunks)]
    there = [exchange(to_z(columns, c, in_tables[m], members)) for c, m in units]
    back = []
    for (c, m), blocks in zip(units, there):
        levels = lax.dynamic_slice_in_dim(eig_z, first + m * chunk, chunk)
        back.append(
            exchange(across(blocks, groups, tables, eig_x, eig_y, levels, shift[c]))
        )
    result = None
    for c in range(count):
        mine = back[c * chunks : (c + 1) * chunks]
        result = from_z(mine, out_table, c, columns.shape, result)
    return result


def solution(mesh):
    in_specs = (P(None, "grp", "pen", None), P(), P(), P(), P(), P(), P(), P(), P(), P(), P(), P())
    out_specs = P(None, "grp", "pen", None)
    return jax.shard_map(
        per_device, mesh=mesh, in_specs=in_specs, out_specs=out_specs, check_vma=False
    )
```

time: 2460 us -> 1530 us (0.62)
  matrix products: 561 us -> 0 us
  local copies, waits for them, and re-layouts: 303 us -> 5.17 us
  waiting for transfers between devices: 1520 us -> 1280 us
  Pallas kernels: 0 us -> 210 us
  starting transfers between devices: 52 us -> 19.3 us
    dot_general x12 -> x0, matrix products: 561 us -> none  [the longest x2 127 us: solve_slab(): back = jnp.einsum('xi,ckij->ckxj', basis_out_x, scaled, precision=highest)]
    all_to_all x8 -> x4, waiting for transfers between devices: 1520 us -> 1280 us  [exchange(): return lax.all_to_all(blocks, BOTH, split_axis=0, concat_axis=0, tiled=True)]
    pallas_call x0 -> x6, Pallas kernels: none -> 210 us  [the longest x2 123 us: planes(): pl.pallas_call(body, grid=(k_size,), in_specs=[block] + [whole(t.shape) f...]
    all_to_all x12 -> x0, local copies, waits for them, and re-layouts: 171 us -> none  [the longest x6 78.1 us: solve_slab(): lax.all_to_all(back, 'grp', split_axis=2, concat_axis=1, tiled=True)]
    dot_general x2 -> x0, local copies, waits for them, and re-layouts: 42 us -> none  [solve_slab(): back = jnp.einsum('yj,ckxj->ckxy', basis_out_y, back, precision=highest)]
    concatenate x1 -> x0, local copies, waits for them, and re-layouts: 37.4 us -> none  [per_device(): return jnp.concatenate(pieces, axis=0)]
    transpose x2 -> x0, local copies, waits for them, and re-layouts: 33.1 us -> none  [solve_slab(): forward = jnp.einsum('kz,cxyz->ckxy', basis_in_z, volume, precision=highest)]
    all_to_all x8 -> x4, starting transfers between devices: 52 us -> 19.3 us  [exchange(): return lax.all_to_all(blocks, BOTH, split_axis=0, concat_axis=0, tiled=True)]
  transfers between devices with their start and end apart: 8 -> 4, of which waited for: 7 -> 4; matrix products, arithmetic and copies ran while one was open for 30% -> 1% of each run, Pallas kernels for 0% -> 11%
where the time goes in v1:
time: 1530 us; the launch traced here: 1520 us
  waiting for transfers between devices  1280 us (84%)
  Pallas kernels  210 us (14%)
  starting transfers between devices  19.3 us (1%)
    all_to_all x4, waiting for transfers between devices, exchange(): return lax.all_to_all(blocks, BOTH, split_axis=0, concat_axis=0, tiled=True)  1280 us
    pallas_call x2, Pallas kernels, planes(): pl.pallas_call(body, grid=(k_size,), in_specs=[block] + [whole(t.shape) f...  123 us
    pallas_call x2, Pallas kernels, z_out(): pl.pallas_call(body, grid=(y_size // ROWS,), in_specs=[pl.BlockSpec((memb...  44.6 us
    pallas_call x2, Pallas kernels, z_in(): pl.pallas_call(body, grid=(y_size // ROWS,), in_specs=[tile(t) for t in r...  42.3 us
  transfers between devices with their start and end apart: 4, of which 4 were waited for; matrix products, arithmetic and copies ran while one was open for 1% of the time, Pallas kernels for 11%

profile of v1, /device:TPU:0, one launch (start us, length us, event | category | flops | bytes accessed | tf_op | source)
XLA Modules:
  0.0 1524.0 jit_solution(11207380226744019631)
XLA Ops:
  0.0 1.4 fusion
  1.4 1.2 pad_maximum_fusion.refs_4_
  2.6 21.2 %shard_map.120 = f32[32,16,64,128]{3,2,1,0:T(8,128)} custom-call(f32[2,128,64,512]{3,2,1,0:T(8,128)} %refs_3_.3, f32[2,128,64,512]{3,2,1,0:T(8,128)} %refs_3_.3, f32[2,128,64,512]{3,2,1,0:T(8,128)} %refs_3_.3, f32[2,128,64,512]{3,2,1,0:T(8,128)} %refs_3_.3, bf16[512,1536]{1,0:T(8,128)(2,1)} %pad_maximum_fusion.refs_4_), custom_call_target="tpu_custom_call" | custom-call | flops 12884901888 | bytes 33554432 | tf_op jit(solution)/shard_map/pallas_call | solution.py:77
  23.9 7.4 all-to-all-start.2
  31.3 21.0 %shard_map.118 = f32[32,16,64,128]{3,2,1,0:T(8,128)} custom-call(f32[2,128,64,512]{3,2,1,0:T(8,128)} %refs_3_.3, f32[2,128,64,512]{3,2,1,0:T(8,128)} %refs_3_.3, f32[2,128,64,512]{3,2,1,0:T(8,128)} %refs_3_.3, f32[2,128,64,512]{3,2,1,0:T(8,128)} %refs_3_.3, bf16[512,1536]{1,0:T(8,128)(2,1)} %pad_maximum_fusion.refs_4_), custom_call_target="tpu_custom_call" | custom-call | flops 12884901888 | bytes 33554432 | tf_op jit(solution)/shard_map/pallas_call | solution.py:77
  52.4 343.6 %all-to-all-done.2.data = f32[32,16,64,128]{3,2,1,0:T(8,128)} async-done(((f32[32,16,64,128]{3,2,1,0:T(8,128)}), f32[32,16,64,128]{3,2,1,0:T(8,128)}, u32[]{:S(2)}, u32[]{:S(2)}) %all-to-all-start.2) | async-done | bytes 16777248 | tf_op jit(solution)/shard_map/all_to_all | solution.py:262
  396.0 3.9 all-to-all-start
  399.9 0.8 copy.19.ey
  401.5 1.4 dynamic_slice.4.ez
  402.9 0.6 gather_fusion
  403.5 0.6 fusion.6
  404.6 0.7 copy-done.5
  405.5 1.8 pad_maximum_fusion.2
  407.3 1.8 pad_maximum_fusion.1
  409.1 61.5 %shard_map.121 = f32[32,16,64,128]{3,2,1,0:T(8,128)} custom-call(f32[32,16,64,128]{3,2,1,0:T(8,128)} %all-to-all-done.2.data, bf16[512,1536]{1,0:T(8,128)(2,1)} %get-tuple-element.19.y_in, bf16[1536,512]{1,0:T(8,128)(2,1)} %get-tuple-element.21.x_in, bf16[1536,512]{1,0:T(8,128)(2,1)} %get-tuple-element.22.x_out, bf16[512,1536]{1,0:T(8,128)(2,1)} %get-tuple-element.20.y_out, ...), custom_call_target="tpu_custom_call" | custom-call | flops 51539607552 | bytes 33554432 | tf_op jit(solution)/shard_map/pallas_call | solution.py:120
  470.6 294.0 %all-to-all-done.data = f32[32,16,64,128]{3,2,1,0:T(8,128)} async-done(((f32[32,16,64,128]{3,2,1,0:T(8,128)}), f32[32,16,64,128]{3,2,1,0:T(8,128)}, u32[]{:S(2)}, u32[]{:S(2)}) %all-to-all-start) | async-done | bytes 16777248 | tf_op jit(solution)/shard_map/all_to_all | solution.py:262
  764.5 3.9 all-to-all-start.3
  768.4 61.4 %shard_map.119 = f32[32,16,64,128]{3,2,1,0:T(8,128)} custom-call(f32[32,16,64,128]{3,2,1,0:T(8,128)} %all-to-all-done.data, bf16[512,1536]{1,0:T(8,128)(2,1)} %get-tuple-element.19.y_in, bf16[1536,512]{1,0:T(8,128)(2,1)} %get-tuple-element.21.x_in, bf16[1536,512]{1,0:T(8,128)(2,1)} %get-tuple-element.22.x_out, bf16[512,1536]{1,0:T(8,128)(2,1)} %get-tuple-element.20.y_out, ...), custom_call_target="tpu_custom_call" | custom-call | flops 51539607552 | bytes 33554432 | tf_op jit(solution)/shard_map/pallas_call | solution.py:120
  829.8 303.3 %all-to-all-done.3.refs_0_ = f32[32,16,64,128]{3,2,1,0:T(8,128)} async-done(((f32[32,16,64,128]{3,2,1,0:T(8,128)}), f32[32,16,64,128]{3,2,1,0:T(8,128)}, u32[]{:S(2)}, u32[]{:S(2)}) %all-to-all-start.3) | async-done | bytes 16777248 | tf_op jit(solution)/shard_map/all_to_all | solution.py:262
  1133.1 4.1 all-to-all-start.1
  1137.7 1.3 pad_maximum_fusion.5.refs_1_
  1139.0 22.3 %shard_map.122.refs_2_ = f32[2,128,64,512]{3,2,1,0:T(8,128)} custom-call(f32[32,16,64,128]{3,2,1,0:T(8,128)} %all-to-all-done.3.refs_0_, bf16[1536,512]{1,0:T(8,128)(2,1)} %pad_maximum_fusion.5.refs_1_), custom_call_target="tpu_custom_call" | custom-call | flops 12884901888 | bytes 33554432 | tf_op jit(solution)/shard_map/pallas_call | solution.py:170
  1161.3 340.4 %all-to-all-done.1.refs_0_ = f32[32,16,64,128]{3,2,1,0:T(8,128)} async-done(((f32[32,16,64,128]{3,2,1,0:T(8,128)}), f32[32,16,64,128]{3,2,1,0:T(8,128)}, u32[]{:S(2)}, u32[]{:S(2)}) %all-to-all-start.1) | async-done | bytes 16777248 | tf_op jit(solution)/shard_map/all_to_all | solution.py:262
  1501.7 22.3 %shard_map.123 = f32[2,128,64,512]{3,2,1,0:T(8,128)} custom-call(f32[32,16,64,128]{3,2,1,0:T(8,128)} %all-to-all-done.1.refs_0_, bf16[1536,512]{1,0:T(8,128)(2,1)} %pad_maximum_fusion.5.refs_1_, f32[2,128,64,512]{3,2,1,0:T(8,128)} %shard_map.122.refs_2_), custom_call_target="tpu_custom_call", output_to_operand_aliasing={{}: (2, {})} | custom-call | flops 12884901888 | bytes 33554432 | tf_op jit(solution)/shard_map/pallas_call | solution.py:170
  (27 shorter events, 1.9 us)
Async XLA Ops:
  0.0 402.9 %copy-start = (f32[64]{0:T(128)S(1)}, f32[64]{0:T(128)}, u32[]{:S(2)}) copy-start(f32[64]{0:T(128)} %param.22) | copy-start | bytes 772
  23.9 372.1 %all-to-all-start.2 = ((f32[32,16,64,128]{3,2,1,0:T(8,128)}), f32[32,16,64,128]{3,2,1,0:T(8,128)}, u32[]{:S(2)}, u32[]{:S(2)}) async-start(f32[32,16,64,128]{3,2,1,0:T(8,128)} %shard_map.120), calls=%async_computation.2 | async-start | bytes 33554432 | tf_op jit(solution)/shard_map/all_to_all | solution.py:262
  52.4 347.5 %copy-start.7 = (f32[512]{0:T(512)S(1)}, f32[512]{0:T(512)}, u32[]{:S(2)}) copy-start(f32[512]{0:T(512)} %param.20) | copy-start | bytes 6148
  52.4 348.4 %copy-start.2 = (f32[512,512]{1,0:T(8,128)S(1)}, f32[512,512]{1,0:T(8,128)}, u32[]{:S(2)}) copy-start(f32[512,512]{1,0:T(8,128)} %param.13) | copy-start | bytes 3145732
  52.4 348.7 %copy-start.3 = (f32[512,512]{1,0:T(8,128)S(1)}, f32[512,512]{1,0:T(8,128)}, u32[]{:S(2)}) copy-start(f32[512,512]{1,0:T(8,128)} %param.16) | copy-start | bytes 3145732
  396.0 368.6 %all-to-all-start = ((f32[32,16,64,128]{3,2,1,0:T(8,128)}), f32[32,16,64,128]{3,2,1,0:T(8,128)}, u32[]{:S(2)}, u32[]{:S(2)}) async-start(f32[32,16,64,128]{3,2,1,0:T(8,128)} %shard_map.118), calls=%async_computation | async-start | bytes 33554432 | tf_op jit(solution)/shard_map/all_to_all | solution.py:262
  399.9 3.0 copy-start.8
  401.5 3.0 copy-start.4
  404.1 1.2 copy-start.5
  764.5 368.6 %all-to-all-start.3 = ((f32[32,16,64,128]{3,2,1,0:T(8,128)}), f32[32,16,64,128]{3,2,1,0:T(8,128)}, u32[]{:S(2)}, u32[]{:S(2)}) async-start(f32[32,16,64,128]{3,2,1,0:T(8,128)} %shard_map.121), calls=%async_computation.3 | async-start | bytes 33554432 | tf_op jit(solution)/shard_map/all_to_all | solution.py:262
  829.8 307.4 %copy-start.6 = (f32[512,512]{1,0:T(8,128)S(1)}, f32[512,512]{1,0:T(8,128)}, u32[]{:S(2)}) copy-start(f32[512,512]{1,0:T(8,128)} %param.18) | copy-start | bytes 3145732
  1133.1 368.6 %all-to-all-start.1 = ((f32[32,16,64,128]{3,2,1,0:T(8,128)}), f32[32,16,64,128]{3,2,1,0:T(8,128)}, u32[]{:S(2)}, u32[]{:S(2)}) async-start(f32[32,16,64,128]{3,2,1,0:T(8,128)} %shard_map.119), calls=%async_computation.1 | async-start | bytes 33554432 | tf_op jit(solution)/shard_map/all_to_all | solution.py:262
  1501.7 22.3 %copy-start.1 = (f32[64]{0:T(128)S(1)}, f32[64]{0:T(128)}, u32[]{:S(2)}) copy-start(f32[64]{0:T(128)} %param.22) | copy-start | bytes 772

commit v2 on v1

v2 whole, which is shorter than its diff:
```python
import jax
import jax.numpy as jnp
from jax import lax
from jax.experimental import pallas as pl
from jax.experimental.pallas import tpu as pltpu
from jax.sharding import PartitionSpec as P

END = 8
LANES = 128
ROWS = 8
VMEM = 56 * 2**20
F32, BF16 = jnp.float32, jnp.bfloat16
BOTH = ("grp", "pen")


def table_parts(table, axis):
    high = lax.reduce_precision(table, exponent_bits=8, mantissa_bits=7)
    low = (table - high).astype(BF16)
    high = high.astype(BF16)
    return jnp.concatenate([high, low, high], axis=axis)


def data_parts(data, axis):
    high = data.astype(BF16)
    low = (data - high.astype(F32)).astype(BF16)
    return jnp.concatenate([high, high, low], axis=axis)


def contract(a, b, dims=((1,), (0,))):
    return lax.dot_general(a, b, (dims, ((), ())), preferred_element_type=F32)


def cost(flops, arrays):
    return pl.CostEstimate(
        flops=flops, bytes_accessed=sum(4 * a.size for a in arrays), transcendentals=0
    )


def params():
    return pltpu.CompilerParams(
        dimension_semantics=("arbitrary",), vmem_limit_bytes=VMEM
    )


def whole(shape):
    return pl.BlockSpec(shape, lambda i: (0,) * len(shape))


def z_in(columns, column, table, members, first, y_size):
    _, x_size, _, length = columns.shape
    rows, triple = table.shape
    part, tiles, skip = rows // members, length // LANES, first // ROWS
    out = jax.ShapeDtypeStruct((members, part, y_size, x_size), F32)

    def body(*refs):
        flat = [r.at[0].reshape(x_size * ROWS, LANES) for r in refs[:tiles]]
        tab, out = refs[tiles], refs[tiles + 1].reshape(rows * ROWS, x_size)
        for y in range(0, ROWS, 2):
            pair = jnp.concatenate(
                [
                    jnp.concatenate(
                        [f[pl.ds(y + d, x_size, stride=ROWS), :] for f in flat], axis=1
                    )
                    for d in range(2)
                ],
                axis=0,
            )
            done = contract(tab[...], data_parts(pair, 1), ((1,), (1,)))
            for d in range(2):
                out[pl.ds(y + d, rows, stride=ROWS), :] = done[
                    :, d * x_size : (d + 1) * x_size
                ]

    def tile(t):
        return pl.BlockSpec(
            (1, x_size, ROWS, LANES), lambda i: (column, 0, i + skip, t)
        )

    return pl.pallas_call(
        body,
        grid=(y_size // ROWS,),
        in_specs=[tile(t) for t in range(tiles)] + [whole(table.shape)],
        out_specs=pl.BlockSpec((members, part, ROWS, x_size), lambda i: (0, 0, i, 0)),
        out_shape=out,
        compiler_params=params(),
        cost_estimate=cost(2 * rows * triple * x_size * y_size, [out, out]),
    )(*[columns] * tiles, table)


def planes(blocks, cuts, groups, tables, eig_x, eig_y, eig_z, shift):
    members, k_size, _, x_size = blocks[0].shape
    slots, count = members // groups, len(blocks)
    y_size = sum(b.shape[2] for b in blocks)
    length = slots * y_size
    triple = 3 * length

    def body(*refs):
        data, out = refs[:count], refs[count + 8 :]
        y_in, x_in, x_out, y_out, ex, ey, ez, sh = refs[count : count + 8]
        plane = jnp.concatenate(
            [
                jnp.concatenate(
                    [d[g * slots + p, 0] for p in range(slots) for d in data], axis=0
                )
                for g in range(groups)
            ],
            axis=1,
        )
        spectral = contract(y_in[...], data_parts(plane, 0))
        spectral = contract(data_parts(spectral, 1), x_in[...])
        value = sh[0]
        root = jnp.sqrt(2.0 * jnp.full((1, length), value, F32))
        denominator = (ex[...] + ey[...]) + (ez[pl.program_id(0)] + value)
        scaled = root * spectral / denominator
        back = contract(data_parts(scaled, 1), x_out[...])
        back = contract(y_out[...], data_parts(back, 0))
        for g in range(groups):
            for p in range(slots):
                start = p * y_size
                for o, cut in zip(out, cuts):
                    o[g * slots + p, 0] = back[
                        start : start + cut, g * x_size : (g + 1) * x_size
                    ]
                    start += cut

    def block(cut):
        return pl.BlockSpec((members, 1, cut, x_size), lambda i: (0, i, 0, 0))

    outs = [jax.ShapeDtypeStruct((members, k_size, cut, x_size), F32) for cut in cuts]
    smem = pl.BlockSpec(memory_space=pltpu.SMEM)
    return pl.pallas_call(
        body,
        grid=(k_size,),
        in_specs=[block(b.shape[2]) for b in blocks]
        + [whole(t.shape) for t in tables]
        + [whole((1, length)), whole((length, 1)), smem, smem],
        out_specs=[block(cut) for cut in cuts],
        out_shape=outs,
        compiler_params=params(),
        cost_estimate=cost(8 * triple * length * length * k_size, [*blocks, *outs]),
    )(
        *blocks,
        *tables,
        eig_x.reshape(1, length),
        eig_y.reshape(length, 1),
        eig_z,
        shift.reshape(1),
    )


def z_out(blocks, table, column, shape, earlier, first):
    members, part, y_size, x_size = blocks.shape
    triple, length = table.shape
    tiles, rows, skip = length // LANES, members * part, first // ROWS

    def body(*refs):
        flat = refs[0].reshape(rows * ROWS, x_size)
        tab, out, turned = refs[1], refs[-2], refs[-1]
        for y in range(0, ROWS, 2):
            pair = jnp.concatenate(
                [flat[pl.ds(y + d, rows, stride=ROWS), :] for d in range(2)], axis=1
            )
            done = contract(data_parts(pair.T, 1), tab[...])
            for d in range(2):
                for t in range(tiles):
                    turned[t, pl.ds(y + d, x_size, stride=ROWS), :] = done[
                        d * x_size : (d + 1) * x_size, t * LANES : (t + 1) * LANES
                    ]
        for t in range(tiles):
            out[0, :, :, t * LANES : (t + 1) * LANES] = turned[t].reshape(
                x_size, ROWS, LANES
            )

    given = [] if earlier is None else [earlier]
    return pl.pallas_call(
        body,
        grid=(y_size // ROWS,),
        in_specs=[
            pl.BlockSpec((members, part, ROWS, x_size), lambda i: (0, 0, i, 0)),
            whole(table.shape),
        ]
        + [pl.BlockSpec(memory_space=pl.ANY)] * len(given),
        out_specs=pl.BlockSpec(
            (1, x_size, ROWS, length), lambda i: (column, 0, i + skip, 0)
        ),
        out_shape=jax.ShapeDtypeStruct(shape, F32),
        scratch_shapes=[pltpu.VMEM((tiles, x_size * ROWS, LANES), F32)],
        input_output_aliases={2: 0} if given else {},
        compiler_params=params(),
        cost_estimate=cost(2 * triple * length * x_size * y_size, [blocks, blocks]),
    )(blocks, table, *given)


def z_in_plain(columns, column, table, members, first, y_size):
    exact = dict(precision=lax.Precision.HIGHEST)
    volume = columns[column, :, first : first + y_size]
    done = jnp.einsum("kz,xyz->kyx", table, volume, **exact)
    return done.reshape(members, -1, *done.shape[1:])


def planes_plain(blocks, cuts, groups, tables, eig_x, eig_y, eig_z, shift):
    exact = dict(precision=lax.Precision.HIGHEST)
    blocks = jnp.concatenate(blocks, axis=2)
    y_in, x_in, x_out, y_out = tables
    members, k_size, y_size, x_size = blocks.shape
    data = blocks.reshape(groups, members // groups, k_size, y_size, x_size)
    plane = data.transpose(2, 1, 3, 0, 4).reshape(
        k_size, members // groups * y_size, groups * x_size
    )
    spectral = jnp.einsum("jy,kyx->kjx", y_in, plane, **exact)
    spectral = jnp.einsum("kjx,xi->kji", spectral, x_in, **exact)
    denominator = eig_x[None, None] + eig_y[None, :, None] + eig_z[:, None, None] + shift
    scaled = jnp.sqrt(2.0 * shift) * spectral / denominator
    back = jnp.einsum("kji,ix->kjx", scaled, x_out, **exact)
    back = jnp.einsum("yj,kjx->kyx", y_out, back, **exact)
    back = back.reshape(k_size, members // groups, y_size, groups, x_size)
    back = back.transpose(3, 1, 0, 2, 4).reshape(blocks.shape)
    return jnp.split(back, [sum(cuts[:i]) for i in range(1, len(cuts))], axis=2)


def z_out_plain(blocks, table, column, shape, earlier, first):
    exact = dict(precision=lax.Precision.HIGHEST)
    rows = blocks.reshape(-1, *blocks.shape[2:])
    done = jnp.einsum("kyx,kz->xyz", rows, table, **exact)
    result = jnp.zeros(shape, F32) if earlier is None else earlier
    return result.at[column, :, first : first + blocks.shape[2]].set(done)


def after(value, *earlier):
    return lax.optimization_barrier((value, *earlier))[0]


def per_device(
    columns,
    basis_in_x,
    basis_in_y,
    basis_in_z,
    basis_out_x,
    basis_out_y,
    basis_out_z,
    eig_x,
    eig_y,
    eig_z,
    shift_table,
    shift_index,
):
    count, x_size, y_size, length = columns.shape
    slots, groups = lax.axis_size("pen"), lax.axis_size("grp")
    members = slots * groups
    k_size = length // members
    shift = shift_table[shift_index]
    tiled = x_size % LANES == 0 and y_size % ROWS == 0 and length % LANES == 0
    parts = table_parts if tiled else lambda table, axis: table
    to_z, across, from_z = (
        (z_in, planes, z_out) if tiled else (z_in_plain, planes_plain, z_out_plain)
    )

    in_table, out_table = parts(basis_in_z, 1), parts(basis_out_z.T, 0)
    tables = [
        parts(basis_in_y, 1),
        parts(basis_in_x.T, 0),
        parts(basis_out_x.T, 0),
        parts(basis_out_y, 1),
    ]
    levels = lax.dynamic_slice_in_dim(
        eig_z, lax.axis_index(BOTH) * k_size, k_size
    )

    def exchange(blocks):
        return lax.all_to_all(blocks, BOTH, split_axis=0, concat_axis=0, tiled=True)

    end = END if tiled and y_size > END else 0
    there = []
    for c in range(count):
        cuts = [end, y_size - end] if end and c == 0 else [y_size]
        sent, first = [], 0
        for cut in cuts:
            table = after(in_table, start) if sent else in_table
            start = to_z(columns, c, table, members, first, cut)
            sent.append(exchange(after(start, sent[-1]) if sent else start))
            first += cut
        there.append(sent)
    back = []
    for c in range(count):
        cuts = [y_size - end, end] if end and c == count - 1 else [y_size]
        outs = across(there[c], cuts, groups, tables, eig_x, eig_y, levels, shift[c])
        got = []
        for out in outs:
            got.append(exchange(after(out, got[-1]) if got else out))
        back.append(got)
    result = None
    for c in range(count):
        first = 0
        for blocks in back[c]:
            result = from_z(blocks, out_table, c, columns.shape, result, first)
            first += blocks.shape[2]
    return result


def solution(mesh):
    in_specs = (P(None, "grp", "pen", None), P(), P(), P(), P(), P(), P(), P(), P(), P(), P(), P())
    out_specs = P(None, "grp", "pen", None)
    return jax.shard_map(
        per_device, mesh=mesh, in_specs=in_specs, out_specs=out_specs, check_vma=False
    )
```

time: 1530 us -> 1510 us (0.987)
  waiting for transfers between devices: 1280 us -> 1250 us
    all_to_all x4 -> x6, waiting for transfers between devices: 1280 us -> 1250 us  [exchange(): return lax.all_to_all(blocks, BOTH, split_axis=0, concat_axis=0, tiled=True)]
    pallas_call x2 -> x3, Pallas kernels: 44.6 us -> 48 us  [z_out(): pl.pallas_call(body, grid=(y_size // ROWS,), in_specs=[pl.BlockSpec((memb...]
    pallas_call x2 -> x3, Pallas kernels: 42.3 us -> 45.5 us  [z_in(): pl.pallas_call(body, grid=(y_size // ROWS,), in_specs=[tile(t) for t in r...]
  transfers between devices with their start and end apart: 4 -> 6, of which waited for: 4 -> 6; matrix products, arithmetic and copies ran while one was open for 1% -> 1% of each run, Pallas kernels for 11% -> 14%
where the time goes in v2:
time: 1510 us
  waiting for transfers between devices  1250 us (83%)
  Pallas kernels  217 us (14%)
  starting transfers between devices  25.6 us (2%)
    all_to_all x6, waiting for transfers between devices, exchange(): return lax.all_to_all(blocks, BOTH, split_axis=0, concat_axis=0, tiled=True)  1250 us
    pallas_call x2, Pallas kernels, planes(): pl.pallas_call(body, grid=(k_size,), in_specs=[block(b.shape[2]) for b in...  123 us
    pallas_call x3, Pallas kernels, z_out(): pl.pallas_call(body, grid=(y_size // ROWS,), in_specs=[pl.BlockSpec((memb...  48 us
    pallas_call x3, Pallas kernels, z_in(): pl.pallas_call(body, grid=(y_size // ROWS,), in_specs=[tile(t) for t in r...  45.5 us
  transfers between devices with their start and end apart: 6, of which 6 were waited for; matrix products, arithmetic and copies ran while one was open for 1% of the time, Pallas kernels for 14%

profile of v2, /device:TPU:0, one launch (start us, length us, event | category | flops | bytes accessed | tf_op | source)
XLA Modules:
  0.0 1511.1 jit_solution(1319510950897753721)
XLA Ops:
  0.0 1.4 fusion
  2.7 5.5 shard_map.120
  8.2 7.3 all-to-all-start.3
  15.5 21.0 %shard_map.118 = f32[32,16,64,128]{3,2,1,0:T(8,128)} custom-call(f32[2,128,64,512]{3,2,1,0:T(8,128)} %refs_3_.5, f32[2,128,64,512]{3,2,1,0:T(8,128)} %refs_3_.5, f32[2,128,64,512]{3,2,1,0:T(8,128)} %refs_3_.5, f32[2,128,64,512]{3,2,1,0:T(8,128)} %refs_3_.5, bf16[512,1536]{1,0:T(8,128)(2,1)} %pad_maximum_fusion.refs_4_), custom_call_target="tpu_custom_call" | custom-call | flops 12884901888 | bytes 33554432 | tf_op jit(solution)/shard_map/pallas_call | solution.py:79
  36.5 29.1 %all-to-all-done.3.refs_0_ = f32[32,16,8,128]{3,2,1,0:T(8,128)S(1)} async-done(((f32[32,16,8,128]{3,2,1,0:T(8,128)}), f32[32,16,8,128]{3,2,1,0:T(8,128)S(1)}, u32[]{:S(2)}, u32[]{:S(2)}) %all-to-all-start.3) | async-done | bytes 2097184 | tf_op jit(solution)/shard_map/all_to_all | solution.py:270
  66.9 3.9 all-to-all-start
  70.8 19.0 %shard_map.121 = f32[32,16,56,128]{3,2,1,0:T(8,128)} custom-call(f32[2,128,64,512]{3,2,1,0:T(8,128)} %refs_3_.5, f32[2,128,64,512]{3,2,1,0:T(8,128)} %refs_3_.5, f32[2,128,64,512]{3,2,1,0:T(8,128)} %refs_3_.5, f32[2,128,64,512]{3,2,1,0:T(8,128)} %refs_3_.5, bf16[512,1536]{1,0:T(8,128)(2,1)} %pad_maximum_fusion.refs_4_), custom_call_target="tpu_custom_call" | custom-call | flops 11274289152 | bytes 29360128 | tf_op jit(solution)/shard_map/pallas_call | solution.py:79
  89.8 345.7 %all-to-all-done.refs_0_ = f32[32,16,64,128]{3,2,1,0:T(8,128)} async-done(((f32[32,16,64,128]{3,2,1,0:T(8,128)}), f32[32,16,64,128]{3,2,1,0:T(8,128)}, u32[]{:S(2)}, u32[]{:S(2)}) %all-to-all-start) | async-done | bytes 16777248 | tf_op jit(solution)/shard_map/all_to_all | solution.py:270
  435.5 3.8 all-to-all-start.4
  445.0 1.8 pad_maximum_fusion.2
  446.8 1.8 pad_maximum_fusion.1
  448.6 61.6 %shard_map.119 = (f32[32,16,56,128]{3,2,1,0:T(8,128)}, f32[32,16,8,128]{3,2,1,0:T(8,128)}) custom-call(f32[32,16,64,128]{3,2,1,0:T(8,128)} %all-to-all-done.refs_0_, bf16[512,1536]{1,0:T(8,128)(2,1)} %get-tuple-element.29.refs_1_.refs_2_, bf16[1536,512]{1,0:T(8,128)(2,1)} %get-tuple-element.31.refs_2_.refs_3_, ...), custom_call_target="tpu_custom_call" | custom-call | flops 51539607552 | bytes 33554432 | tf_op jit(solution)/shard_map/pallas_call | solution.py:131
  510.2 248.9 %all-to-all-done.4.refs_1_ = f32[32,16,56,128]{3,2,1,0:T(8,128)} async-done(((f32[32,16,56,128]{3,2,1,0:T(8,128)}), f32[32,16,56,128]{3,2,1,0:T(8,128)}, u32[]{:S(2)}, u32[]{:S(2)}) %all-to-all-start.4) | async-done | bytes 14680096 | tf_op jit(solution)/shard_map/all_to_all | solution.py:270
  759.1 4.0 all-to-all-start.1
  763.1 61.6 %shard_map.122 = f32[32,16,64,128]{3,2,1,0:T(8,128)} custom-call(f32[32,16,8,128]{3,2,1,0:T(8,128)} %copy-done.3, f32[32,16,56,128]{3,2,1,0:T(8,128)} %all-to-all-done.4.refs_1_, bf16[512,1536]{1,0:T(8,128)(2,1)} %get-tuple-element.29.refs_1_.refs_2_, bf16[1536,512]{1,0:T(8,128)(2,1)} %get-tuple-element.31.refs_2_.refs_3_, ...), custom_call_target="tpu_custom_call" | custom-call | flops 51539607552 | bytes 33554432 | tf_op jit(solution)/shard_map/pallas_call | solution.py:131
  824.6 258.0 %all-to-all-done.1.refs_0_ = f32[32,16,56,128]{3,2,1,0:T(8,128)} async-done(((f32[32,16,56,128]{3,2,1,0:T(8,128)}), f32[32,16,56,128]{3,2,1,0:T(8,128)}, u32[]{:S(2)}, u32[]{:S(2)}) %all-to-all-start.1) | async-done | bytes 14680096 | tf_op jit(solution)/shard_map/all_to_all | solution.py:270
  1082.6 3.9 all-to-all-start.5
  1086.5 364.7 %all-to-all-done.5.refs_0_ = f32[32,16,64,128]{3,2,1,0:T(8,128)} async-done(((f32[32,16,64,128]{3,2,1,0:T(8,128)}), f32[32,16,64,128]{3,2,1,0:T(8,128)}, u32[]{:S(2)}, u32[]{:S(2)}) %all-to-all-start.5) | async-done | bytes 16777248 | tf_op jit(solution)/shard_map/all_to_all | solution.py:270
  1451.2 2.7 all-to-all-start.2
  1453.9 1.6 copy.21
  1457.0 22.3 %shard_map.123.refs_2_ = f32[2,128,64,512]{3,2,1,0:T(8,128)} custom-call(f32[32,16,64,128]{3,2,1,0:T(8,128)} %all-to-all-done.5.refs_0_, bf16[1536,512]{1,0:T(8,128)(2,1)} %pad_maximum_fusion.5.refs_1_), custom_call_target="tpu_custom_call" | custom-call | flops 12884901888 | bytes 33554432 | tf_op jit(solution)/shard_map/pallas_call | solution.py:175
  1479.3 19.9 %shard_map.124.refs_2_ = f32[2,128,64,512]{3,2,1,0:T(8,128)} custom-call(f32[32,16,56,128]{3,2,1,0:T(8,128)} %all-to-all-done.1.refs_0_, bf16[1536,512]{1,0:T(8,128)(2,1)} %pad_maximum_fusion.5.refs_1_, f32[2,128,64,512]{3,2,1,0:T(8,128)} %shard_map.123.refs_2_), custom_call_target="tpu_custom_call", output_to_operand_aliasing={{}: (2, {})} | custom-call | flops 11274289152 | bytes 29360128 | tf_op jit(solution)/shard_map/pallas_call | solution.py:175
  1499.2 4.8 all-to-all-done.2.refs_0_
  1505.4 5.7 shard_map.125
  (35 shorter events, 11.0 us)
Async XLA Ops:
  0.0 442.3 %copy-start = (f32[64]{0:T(128)S(1)}, f32[64]{0:T(128)}, u32[]{:S(2)}) copy-start(f32[64]{0:T(128)} %param.22) | copy-start | bytes 772
  8.2 57.4 %all-to-all-start.3 = ((f32[32,16,8,128]{3,2,1,0:T(8,128)}), f32[32,16,8,128]{3,2,1,0:T(8,128)S(1)}, u32[]{:S(2)}, u32[]{:S(2)}) async-start(f32[32,16,8,128]{3,2,1,0:T(8,128)} %shard_map.120), calls=%async_computation.3 | async-start | bytes 4194304 | tf_op jit(solution)/shard_map/all_to_all | solution.py:270
  65.6 1.4 copy-start.3
  66.9 368.6 %all-to-all-start = ((f32[32,16,64,128]{3,2,1,0:T(8,128)}), f32[32,16,64,128]{3,2,1,0:T(8,128)}, u32[]{:S(2)}, u32[]{:S(2)}) async-start(f32[32,16,64,128]{3,2,1,0:T(8,128)} %shard_map.118), calls=%async_computation | async-start | bytes 33554432 | tf_op jit(solution)/shard_map/all_to_all | solution.py:270
  89.8 349.6 %copy-start.8 = (f32[512]{0:T(512)S(1)}, f32[512]{0:T(512)}, u32[]{:S(2)}) copy-start(f32[512]{0:T(512)} %param.20) | copy-start | bytes 6148
  89.8 350.4 %copy-start.4 = (f32[512,512]{1,0:T(8,128)S(1)}, f32[512,512]{1,0:T(8,128)}, u32[]{:S(2)}) copy-start(f32[512,512]{1,0:T(8,128)} %param.13) | copy-start | bytes 3145732
  89.8 350.8 %copy-start.5 = (f32[512,512]{1,0:T(8,128)S(1)}, f32[512,512]{1,0:T(8,128)}, u32[]{:S(2)}) copy-start(f32[512,512]{1,0:T(8,128)} %param.16) | copy-start | bytes 3145732
  435.5 323.6 %all-to-all-start.4 = ((f32[32,16,56,128]{3,2,1,0:T(8,128)}), f32[32,16,56,128]{3,2,1,0:T(8,128)}, u32[]{:S(2)}, u32[]{:S(2)}) async-start(f32[32,16,56,128]{3,2,1,0:T(8,128)} %shard_map.121), calls=%async_computation.4 | async-start | bytes 29360128 | tf_op jit(solution)/shard_map/all_to_all | solution.py:270
  439.3 3.0 copy-start.9
  440.9 3.0 copy-start.6
  443.6 1.2 copy-start.7
  759.1 323.6 %all-to-all-start.1 = ((f32[32,16,56,128]{3,2,1,0:T(8,128)}), f32[32,16,56,128]{3,2,1,0:T(8,128)}, u32[]{:S(2)}, u32[]{:S(2)}) async-start(f32[32,16,56,128]{3,2,1,0:T(8,128)} %get-tuple-element.11), calls=%async_computation.1 | async-start | bytes 29360128 | tf_op jit(solution)/shard_map/all_to_all | solution.py:270
  1082.6 368.6 %all-to-all-start.5 = ((f32[32,16,64,128]{3,2,1,0:T(8,128)}), f32[32,16,64,128]{3,2,1,0:T(8,128)}, u32[]{:S(2)}, u32[]{:S(2)}) async-start(f32[32,16,64,128]{3,2,1,0:T(8,128)} %shard_map.122), calls=%async_computation.5 | async-start | bytes 33554432 | tf_op jit(solution)/shard_map/all_to_all | solution.py:270
  1451.2 52.8 %all-to-all-start.2 = ((f32[32,16,8,128]{3,2,1,0:T(8,128)}), f32[32,16,8,128]{3,2,1,0:T(8,128)S(1)}, u32[]{:S(2)}, u32[]{:S(2)}) async-start(f32[32,16,8,128]{3,2,1,0:T(8,128)} %get-tuple-element.12), calls=%async_computation.2 | async-start | bytes 4194304 | tf_op jit(solution)/shard_map/all_to_all | solution.py:270
  1504.1 1.3 copy-start.2
  1505.4 5.7 copy-start.1

commit v3 on v2

--- a/solution.py
+++ b/solution.py
@@ -5,7 +5,7 @@
 from jax.experimental.pallas import tpu as pltpu
 from jax.sharding import PartitionSpec as P
 
-END = 8
+LATE = 4
 LANES = 128
 ROWS = 8
 VMEM = 56 * 2**20
@@ -87,7 +87,65 @@
     )(*[columns] * tiles, table)
 
 
-def planes(blocks, cuts, groups, tables, eig_x, eig_y, eig_z, shift):
+def z_in_first(columns, table, me, groups, slots):
+    _, x_size, _, length = columns.shape
+    k_size, tiles = length // (groups * slots), length // LANES
+    share = groups * k_size
+    outs = [jax.ShapeDtypeStruct((groups, k_size, ROWS, x_size), F32)] * slots
+
+    def body(*refs):
+        flat = [r.at[0].reshape(x_size * ROWS, LANES) for r in refs[:tiles]]
+        tab, place = refs[tiles], refs[tiles + 1]
+        out = [r.reshape(share * ROWS, x_size) for r in refs[tiles + 2 :]]
+
+        def row(s, t):
+            member = (place[0] ^ t) * slots + (place[1] ^ s)
+            return pl.multiple_of(member * k_size, ROWS)
+
+        ordered = jnp.concatenate(
+            [
+                tab[pl.ds(row(s, t), k_size), :]
+                for s in range(slots)
+                for t in range(groups)
+            ],
+            axis=0,
+        )
+        high = ordered.astype(BF16)
+        low = (ordered - high.astype(F32)).astype(BF16)
+        ordered = jnp.concatenate([high, low, high], axis=1)
+        for y in range(0, ROWS, 2):
+            pair = jnp.concatenate(
+                [
+                    jnp.concatenate(
+                        [f[pl.ds(y + d, x_size, stride=ROWS), :] for f in flat], axis=1
+                    )
+                    for d in range(2)
+                ],
+                axis=0,
+            )
+            done = contract(ordered, data_parts(pair, 1), ((1,), (1,)))
+            for n, o in enumerate(out):
+                for d in range(2):
+                    o[pl.ds(y + d, share, stride=ROWS), :] = done[
+                        n * share : (n + 1) * share, d * x_size : (d + 1) * x_size
+                    ]
+
+    def tile(t):
+        return pl.BlockSpec((1, x_size, ROWS, LANES), lambda i: (0, 0, 0, t))
+
+    return pl.pallas_call(
+        body,
+        grid=(1,),
+        in_specs=[tile(t) for t in range(tiles)]
+        + [whole(table.shape), pl.BlockSpec(memory_space=pltpu.SMEM)],
+        out_specs=[whole(o.shape) for o in outs],
+        out_shape=outs,
+        compiler_params=params(),
+        cost_estimate=cost(6 * length * length * x_size * ROWS, [*outs, *outs]),
+    )(*[columns] * tiles, table, me)
+
+
+def planes(blocks, cuts, slotted, me, groups, tables, eig_x, eig_y, eig_z, shift):
     members, k_size, _, x_size = blocks[0].shape
     slots, count = members // groups, len(blocks)
     y_size = sum(b.shape[2] for b in blocks)
@@ -95,12 +153,23 @@
     triple = 3 * length
 
     def body(*refs):
-        data, out = refs[:count], refs[count + 8 :]
-        y_in, x_in, x_out, y_out, ex, ey, ez, sh = refs[count : count + 8]
+        data, out = refs[:count], refs[count + 9 :]
+        y_in, x_in, x_out, y_out, ex, ey, ez, sh, place = refs[count : count + 9]
+
+        def index(g, p, size):
+            if size in slotted:
+                return (place[0] ^ g) * slots + (place[1] ^ p)
+            return g * slots + p
+
         plane = jnp.concatenate(
             [
                 jnp.concatenate(
-                    [d[g * slots + p, 0] for p in range(slots) for d in data], axis=0
+                    [
+                        d[index(g, p, d.shape[2]), 0]
+                        for p in range(slots)
+                        for d in data
+                    ],
+                    axis=0,
                 )
                 for g in range(groups)
             ],
@@ -118,7 +187,7 @@
             for p in range(slots):
                 start = p * y_size
                 for o, cut in zip(out, cuts):
-                    o[g * slots + p, 0] = back[
+                    o[index(g, p, cut), 0] = back[
                         start : start + cut, g * x_size : (g + 1) * x_size
                     ]
                     start += cut
@@ -133,7 +202,7 @@
         grid=(k_size,),
         in_specs=[block(b.shape[2]) for b in blocks]
         + [whole(t.shape) for t in tables]
-        + [whole((1, length)), whole((length, 1)), smem, smem],
+        + [whole((1, length)), whole((length, 1)), smem, smem, smem],
         out_specs=[block(cut) for cut in cuts],
         out_shape=outs,
         compiler_params=params(),
@@ -145,20 +214,28 @@
         eig_y.reshape(length, 1),
         eig_z,
         shift.reshape(1),
+        me,
     )
 
 
 def z_out(blocks, table, column, shape, earlier, first):
-    members, part, y_size, x_size = blocks.shape
+    count = len(blocks)
+    members, part, y_size, x_size = blocks[0].shape
     triple, length = table.shape
     tiles, rows, skip = length // LANES, members * part, first // ROWS
 
     def body(*refs):
-        flat = refs[0].reshape(rows * ROWS, x_size)
-        tab, out, turned = refs[1], refs[-2], refs[-1]
+        flat = [r.reshape(rows * ROWS, x_size) for r in refs[:count]]
+        tab, out, turned = refs[count], refs[-2], refs[-1]
         for y in range(0, ROWS, 2):
             pair = jnp.concatenate(
-                [flat[pl.ds(y + d, rows, stride=ROWS), :] for d in range(2)], axis=1
+                [
+                    jnp.concatenate(
+                        [f[pl.ds(y + d, rows, stride=ROWS), :] for f in flat], axis=0
+                    )
+                    for d in range(2)
+                ],
+                axis=1,
             )
             done = contract(data_parts(pair.T, 1), tab[...])
             for d in range(2):
@@ -175,20 +252,19 @@
     return pl.pallas_call(
         body,
         grid=(y_size // ROWS,),
-        in_specs=[
-            pl.BlockSpec((members, part, ROWS, x_size), lambda i: (0, 0, i, 0)),
-            whole(table.shape),
-        ]
+        in_specs=[pl.BlockSpec((members, part, ROWS, x_size), lambda i: (0, 0, i, 0))]
+        * count
+        + [whole(table.shape)]
         + [pl.BlockSpec(memory_space=pl.ANY)] * len(given),
         out_specs=pl.BlockSpec(
             (1, x_size, ROWS, length), lambda i: (column, 0, i + skip, 0)
         ),
         out_shape=jax.ShapeDtypeStruct(shape, F32),
         scratch_shapes=[pltpu.VMEM((tiles, x_size * ROWS, LANES), F32)],
-        input_output_aliases={2: 0} if given else {},
+        input_output_aliases={count + 1: 0} if given else {},
         compiler_params=params(),
-        cost_estimate=cost(2 * triple * length * x_size * y_size, [blocks, blocks]),
-    )(blocks, table, *given)
+        cost_estimate=cost(2 * triple * length * x_size * y_size, [*blocks, *blocks]),
+    )(*blocks, table, *given)
 
 
 def z_in_plain(columns, column, table, members, first, y_size):
@@ -198,7 +274,7 @@
     return done.reshape(members, -1, *done.shape[1:])
 
 
-def planes_plain(blocks, cuts, groups, tables, eig_x, eig_y, eig_z, shift):
+def planes_plain(blocks, cuts, slotted, me, groups, tables, eig_x, eig_y, eig_z, shift):
     exact = dict(precision=lax.Precision.HIGHEST)
     blocks = jnp.concatenate(blocks, axis=2)
     y_in, x_in, x_out, y_out = tables
@@ -220,6 +296,7 @@
 
 def z_out_plain(blocks, table, column, shape, earlier, first):
     exact = dict(precision=lax.Precision.HIGHEST)
+    (blocks,) = blocks
     rows = blocks.reshape(-1, *blocks.shape[2:])
     done = jnp.einsum("kyx,kz->xyz", rows, table, **exact)
     result = jnp.zeros(shape, F32) if earlier is None else earlier
@@ -228,6 +305,24 @@
 
 def after(value, *earlier):
     return lax.optimization_barrier((value, *earlier))[0]
+
+
+def slot_order(table, axis, mesh_axis):
+    order = lax.axis_index(mesh_axis) ^ jnp.arange(lax.axis_size(mesh_axis))
+    return jnp.take(table, order, axis=axis, mode="clip")
+
+
+def swap(blocks, axis):
+    size = len(blocks)
+    far = sorted(range(1, size), key=lambda s: s < size // 2)
+    got = {0: blocks[0]}
+    for s in far:
+        got[s] = lax.ppermute(blocks[s], axis, [(m, m ^ s) for m in range(size)])
+    return [got[s] for s in range(size)]
+
+
+def turn(blocks):
+    return [jnp.stack([b[n] for b in blocks]) for n in range(blocks[0].shape[0])]
 
 
 def per_device(
@@ -262,38 +357,57 @@
         parts(basis_out_x.T, 0),
         parts(basis_out_y, 1),
     ]
+
+    def by_member(table):
+        table = table.reshape(groups, slots, k_size, length)
+        table = slot_order(slot_order(table, 0, "grp"), 1, "pen")
+        return table.transpose(1, 0, 2, 3).reshape(length, length)
+
+    slot_out_table = parts(by_member(basis_out_z.T), 0)
+    me = jnp.stack([lax.axis_index("grp"), lax.axis_index("pen")])
     levels = lax.dynamic_slice_in_dim(
         eig_z, lax.axis_index(BOTH) * k_size, k_size
     )
 
-    def exchange(blocks):
-        return lax.all_to_all(blocks, BOTH, split_axis=0, concat_axis=0, tiled=True)
-
-    end = END if tiled and y_size > END else 0
-    there = []
+    def exchange(block):
+        return lax.all_to_all(block, BOTH, split_axis=0, concat_axis=0, tiled=True)
+
+    end = ROWS if tiled and y_size > ROWS and k_size % ROWS == 0 else 0
+    there, previous = [], None
     for c in range(count):
-        cuts = [end, y_size - end] if end and c == 0 else [y_size]
-        sent, first = [], 0
-        for cut in cuts:
-            table = after(in_table, start) if sent else in_table
-            start = to_z(columns, c, table, members, first, cut)
-            sent.append(exchange(after(start, sent[-1]) if sent else start))
-            first += cut
-        there.append(sent)
-    back = []
+        blocks, first = [], 0
+        if end and c == 0:
+            small = z_in_first(columns, basis_in_z, me, groups, slots)
+            small = swap(small, "pen")
+            previous = small[1:]
+            small = swap(turn(small), "grp")
+            blocks, first = [jnp.concatenate(small)], end
+        table = after(in_table, *small[1:]) if end and c == 1 else in_table
+        out = to_z(columns, c, table, members, first, y_size - first)
+        out = exchange(after(out, *previous) if previous else out)
+        previous = [out]
+        there.append([*blocks, out])
+    back, previous = [], None
     for c in range(count):
-        cuts = [y_size - end, end] if end and c == count - 1 else [y_size]
-        outs = across(there[c], cuts, groups, tables, eig_x, eig_y, levels, shift[c])
-        got = []
-        for out in outs:
-            got.append(exchange(after(out, got[-1]) if got else out))
-        back.append(got)
+        cuts = [end, y_size - end] if end and c == count - 1 else [y_size]
+        outs = across(
+            there[c], cuts, [end], me, groups, tables, eig_x, eig_y, levels, shift[c]
+        )
+        out = exchange(after(outs[-1], *previous) if previous else outs[-1])
+        previous = [out]
+        back.append([(y_size - cuts[-1], [out], out_table)])
+        if len(cuts) > 1:
+            small = outs[0].reshape(groups, slots, *outs[0].shape[1:])
+            small = turn(swap([small[t] for t in range(groups)], "grp"))
+            late = slots - slots // LATE
+            small = swap(
+                [after(b, out) if s >= late else b for s, b in enumerate(small)], "pen"
+            )
+            back[c].append((0, small, slot_out_table))
     result = None
     for c in range(count):
-        first = 0
-        for blocks in back[c]:
-            result = from_z(blocks, out_table, c, columns.shape, result, first)
-            first += blocks.shape[2]
+        for first, blocks, table in back[c]:
+            result = from_z(blocks, table, c, columns.shape, result, first)
     return result
 
 

time: 1510 us -> 1490 us (0.987)
  waiting for transfers between devices: 1250 us -> 1160 us
  starting transfers between devices: 25.6 us -> 76 us
    all_to_all x6 -> x4, waiting for transfers between devices: 1250 us -> 899 us  [exchange(): return lax.all_to_all(block, BOTH, split_axis=0, concat_axis=0, tiled=True)]
    ppermute x0 -> x20, waiting for transfers between devices: none -> 264 us  [swap(): got[s] = lax.ppermute(blocks[s], axis, [(m, m ^ s) for m in range(size)])]
    ppermute x0 -> x20, starting transfers between devices: none -> 48 us  [swap(): got[s] = lax.ppermute(blocks[s], axis, [(m, m ^ s) for m in range(size)])]
    pallas_call x3 -> x2, Pallas kernels: 45.5 us -> 40 us  [z_in(): pl.pallas_call(body, grid=(y_size // ROWS,), in_specs=[tile(t) for t in r...]
  transfers between devices with their start and end apart: 6 -> 24, of which waited for: 6 -> 9; matrix products, arithmetic and copies ran while one was open for 1% -> 2% of each run, Pallas kernels for 14% -> 14%
where the time goes in v3:
time: 1490 us
  waiting for transfers between devices  1160 us (78%)
  Pallas kernels  217 us (15%)
  starting transfers between devices  76 us (5%)
  local copies, waits for them, and re-layouts  19.4 us (1%)
    all_to_all x4, waiting for transfers between devices, exchange(): return lax.all_to_all(block, BOTH, split_axis=0, concat_axis=0, tiled=True)  899 us
    ppermute x20, waiting for transfers between devices, swap(): got[s] = lax.ppermute(blocks[s], axis, [(m, m ^ s) for m in range(size)])  264 us
    pallas_call x2, Pallas kernels, planes(): pl.pallas_call(body, grid=(k_size,), in_specs=[block(b.shape[2]) for b in...  124 us
    ppermute x20, starting transfers between devices, swap(): got[s] = lax.ppermute(blocks[s], axis, [(m, m ^ s) for m in range(size)])  48 us
    pallas_call x3, Pallas kernels, z_out(): pl.pallas_call(body, grid=(y_size // ROWS,), in_specs=[pl.BlockSpec((memb...  48 us
    pallas_call x2, Pallas kernels, z_in(): pl.pallas_call(body, grid=(y_size // ROWS,), in_specs=[tile(t) for t in r...  40 us
  transfers between devices with their start and end apart: 24, of which 9 were waited for; matrix products, arithmetic and copies ran while one was open for 2% of the time, Pallas kernels for 14%

profile of v3, /device:TPU:0, one launch (start us, length us, event | category | flops | bytes accessed | tf_op | source)
XLA Modules:
  0.0 1485.3 jit_solution(10883144825676693112)
XLA Ops:
  0.6 5.3 shard_map.118
  13.2 3.6 collective-permute-start.5
  16.8 10.3 collective-permute-done.1
  27.7 19.0 %shard_map.120 = f32[32,16,56,128]{3,2,1,0:T(8,128)} custom-call(f32[2,128,64,512]{3,2,1,0:T(8,128)} %refs_3_.5, f32[2,128,64,512]{3,2,1,0:T(8,128)} %refs_3_.5, f32[2,128,64,512]{3,2,1,0:T(8,128)} %refs_3_.5, f32[2,128,64,512]{3,2,1,0:T(8,128)} %refs_3_.5, bf16[512,1536]{1,0:T(8,128)(2,1)} %pad_maximum_fusion.refs_4_), custom_call_target="tpu_custom_call" | custom-call | flops 11274289152 | bytes 29360128 | tf_op jit(solution)/shard_map/pallas_call | solution.py:79
  46.7 16.0 %all-to-all-start = ((f32[32,16,56,128]{3,2,1,0:T(8,128)}), f32[32,16,56,128]{3,2,1,0:T(8,128)}, u32[]{:S(2)}, u32[]{:S(2)}) async-start(f32[32,16,56,128]{3,2,1,0:T(8,128)} %shard_map.120), calls=%async_computation | async-start | bytes 29360128 | tf_op jit(solution)/shard_map/all_to_all | solution.py:373
  71.3 126.9 %collective-permute-done.9 = f32[8,16,8,128]{3,2,1,0:T(8,128)} collective-permute-done((f32[8,16,8,128]{3,2,1,0:T(8,128)S(1)}, f32[8,16,8,128]{3,2,1,0:T(8,128)}, u32[]{:S(2)}, u32[]{:S(2)}) %collective-permute-start.9) | collective-permute-done | bytes 524320 | tf_op jit(solution)/shard_map/ppermute | solution.py:320
  198.3 12.3 collective-permute-done.7
  210.5 21.0 %shard_map.119 = f32[32,16,64,128]{3,2,1,0:T(8,128)} custom-call(f32[2,128,64,512]{3,2,1,0:T(8,128)} %refs_3_.5, f32[2,128,64,512]{3,2,1,0:T(8,128)} %refs_3_.5, f32[2,128,64,512]{3,2,1,0:T(8,128)} %refs_3_.5, f32[2,128,64,512]{3,2,1,0:T(8,128)} %refs_3_.5, bf16[512,1536]{1,0:T(8,128)(2,1)} %pad_maximum_fusion.refs_4_), custom_call_target="tpu_custom_call" | custom-call | flops 12884901888 | bytes 33554432 | tf_op jit(solution)/shard_map/pallas_call | solution.py:79
  231.5 150.9 %all-to-all-done.refs_1_ = f32[32,16,56,128]{3,2,1,0:T(8,128)} async-done(((f32[32,16,56,128]{3,2,1,0:T(8,128)}), f32[32,16,56,128]{3,2,1,0:T(8,128)}, u32[]{:S(2)}, u32[]{:S(2)}) %all-to-all-start) | async-done | bytes 14680096 | tf_op jit(solution)/shard_map/all_to_all | solution.py:373
  382.4 3.9 all-to-all-start.1
  401.5 61.9 %shard_map.122 = f32[32,16,64,128]{3,2,1,0:T(8,128)} custom-call(f32[32,16,8,128]{3,2,1,0:T(8,128)} %copy-done.19, f32[32,16,56,128]{3,2,1,0:T(8,128)} %all-to-all-done.refs_1_, bf16[512,1536]{1,0:T(8,128)(2,1)} %get-tuple-element.122.refs_1_.refs_2_, bf16[1536,512]{1,0:T(8,128)(2,1)} %get-tuple-element.124.refs_2_.refs_3_, ...), custom_call_target="tpu_custom_call" | custom-call | flops 51539607552 | bytes 33554432 | tf_op jit(solution)/shard_map/pallas_call | solution.py:200
  463.4 287.6 %all-to-all-done.1.refs_0_ = f32[32,16,64,128]{3,2,1,0:T(8,128)} async-done(((f32[32,16,64,128]{3,2,1,0:T(8,128)}), f32[32,16,64,128]{3,2,1,0:T(8,128)}, u32[]{:S(2)}, u32[]{:S(2)}) %all-to-all-start.1) | async-done | bytes 16777248 | tf_op jit(solution)/shard_map/all_to_all | solution.py:373
  751.0 4.1 all-to-all-start.2
  755.1 61.8 %shard_map.121 = (f32[32,16,8,128]{3,2,1,0:T(8,128)}, f32[32,16,56,128]{3,2,1,0:T(8,128)}) custom-call(f32[32,16,64,128]{3,2,1,0:T(8,128)} %all-to-all-done.1.refs_0_, bf16[512,1536]{1,0:T(8,128)(2,1)} %get-tuple-element.122.refs_1_.refs_2_, bf16[1536,512]{1,0:T(8,128)(2,1)} %get-tuple-element.124.refs_2_.refs_3_, ...), custom_call_target="tpu_custom_call" | custom-call | flops 51539607552 | bytes 33554432 | tf_op jit(solution)/shard_map/pallas_call | solution.py:200
  816.9 302.7 %all-to-all-done.2.refs_0_ = f32[32,16,64,128]{3,2,1,0:T(8,128)} async-done(((f32[32,16,64,128]{3,2,1,0:T(8,128)}), f32[32,16,64,128]{3,2,1,0:T(8,128)}, u32[]{:S(2)}, u32[]{:S(2)}) %all-to-all-start.2) | async-done | bytes 16777248 | tf_op jit(solution)/shard_map/all_to_all | solution.py:373
  1119.6 4.0 all-to-all-start.3
  1131.8 22.3 %shard_map.123.refs_2_ = f32[2,128,64,512]{3,2,1,0:T(8,128)} custom-call(f32[32,16,64,128]{3,2,1,0:T(8,128)} %all-to-all-done.2.refs_0_, bf16[1536,512]{1,0:T(8,128)(2,1)} %pad_maximum_fusion.6.refs_1_), custom_call_target="tpu_custom_call" | custom-call | flops 12884901888 | bytes 33554432 | tf_op jit(solution)/shard_map/pallas_call | solution.py:252
  1154.1 93.1 %collective-permute-done.10 = f32[8,16,8,128]{3,2,1,0:T(8,128)S(1)} collective-permute-done((f32[8,16,8,128]{3,2,1,0:T(8,128)S(1)}, f32[8,16,8,128]{3,2,1,0:T(8,128)S(1)}, u32[]{:S(2)}, u32[]{:S(2)}) %collective-permute-start.10) | collective-permute-done | bytes 524320 | tf_op jit(solution)/shard_map/ppermute | solution.py:320
  1247.3 21.2 %collective-permute-done.12 = f32[8,16,8,128]{3,2,1,0:T(8,128)S(1)} collective-permute-done((f32[8,16,8,128]{3,2,1,0:T(8,128)S(1)}, f32[8,16,8,128]{3,2,1,0:T(8,128)S(1)}, u32[]{:S(2)}, u32[]{:S(2)}) %collective-permute-start.12) | collective-permute-done | bytes 524320 | tf_op jit(solution)/shard_map/ppermute | solution.py:320
  1270.8 25.5 %collective-permute-start.16 = (f32[4,16,8,128]{3,2,1,0:T(8,128)S(1)}, f32[4,16,8,128]{3,2,1,0:T(8,128)S(1)}, u32[]{:S(2)}, u32[]{:S(2)}) collective-permute-start(f32[4,16,8,128]{3,2,1,0:T(8,128)S(1)} %pad_maximum_fusion.11), channel_id=1, source_target_pairs={{0,4},{1,5},{2,6},{3,7},{4,0},{5,1},{6,2},{7,3},{8,12},{9,13},{10,... | collective-permute-start | bytes 786440 | tf_op jit(solution)/shard_map/ppermute | solution.py:320
  1297.2 157.4 %all-to-all-done.3.refs_0_ = f32[32,16,56,128]{3,2,1,0:T(8,128)} async-done(((f32[32,16,56,128]{3,2,1,0:T(8,128)}), f32[32,16,56,128]{3,2,1,0:T(8,128)}, u32[]{:S(2)}, u32[]{:S(2)}) %all-to-all-start.3) | async-done | bytes 14680096 | tf_op jit(solution)/shard_map/all_to_all | solution.py:373
  1454.6 3.2 collective-permute-start.19
  1457.9 20.0 %shard_map.124.refs_9_ = f32[2,128,64,512]{3,2,1,0:T(8,128)} custom-call(f32[32,16,56,128]{3,2,1,0:T(8,128)} %all-to-all-done.3.refs_0_, bf16[1536,512]{1,0:T(8,128)(2,1)} %pad_maximum_fusion.6.refs_1_, f32[2,128,64,512]{3,2,1,0:T(8,128)} %shard_map.123.refs_2_), custom_call_target="tpu_custom_call", output_to_operand_aliasing={{}: (2, {})} | custom-call | flops 11274289152 | bytes 29360128 | tf_op jit(solution)/shard_map/pallas_call | solution.py:252
  1479.5 5.7 shard_map.125
  (129 shorter events, 45.2 us)
Async XLA Ops:
  5.9 7.3 collective-permute-start
  6.3 20.7 %collective-permute-start.1 = (f32[4,16,8,128]{3,2,1,0:T(8,128)}, f32[4,16,8,128]{3,2,1,0:T(8,128)S(1)}, u32[]{:S(2)}, u32[]{:S(2)}) collective-permute-start(f32[4,16,8,128]{3,2,1,0:T(8,128)} %get-tuple-element.23), channel_id=1, source_target_pairs={{0,2},{1,3},{2,0},{3,1},{4,6},{5,7},{6,4},{7,5},{8,10},{9,11},{10,... | collective-permute-start | bytes 786440 | tf_op jit(solution)/shard_map/ppermute | solution.py:320
  8.9 37.7 %collective-permute-start.2 = (f32[4,16,8,128]{3,2,1,0:T(8,128)}, f32[4,16,8,128]{3,2,1,0:T(8,128)S(1)}, u32[]{:S(2)}, u32[]{:S(2)}) collective-permute-start(f32[4,16,8,128]{3,2,1,0:T(8,128)} %get-tuple-element.24), channel_id=1, source_target_pairs={{0,3},{1,2},{2,1},{3,0},{4,7},{5,6},{6,5},{7,4},{8,11},{9,10},{10,... | collective-permute-start | bytes 786440 | tf_op jit(solution)/shard_map/ppermute | solution.py:320
  9.1 37.6 %collective-permute-start.3 = (f32[4,16,8,128]{3,2,1,0:T(8,128)}, f32[4,16,8,128]{3,2,1,0:T(8,128)S(1)}, u32[]{:S(2)}, u32[]{:S(2)}) collective-permute-start(f32[4,16,8,128]{3,2,1,0:T(8,128)} %get-tuple-element.25), channel_id=1, source_target_pairs={{0,4},{1,5},{2,6},{3,7},{4,0},{5,1},{6,2},{7,3},{8,12},{9,13},{10,... | collective-permute-start | bytes 786440 | tf_op jit(solution)/shard_map/ppermute | solution.py:320
  11.8 34.9 %collective-permute-start.4 = (f32[4,16,8,128]{3,2,1,0:T(8,128)}, f32[4,16,8,128]{3,2,1,0:T(8,128)S(1)}, u32[]{:S(2)}, u32[]{:S(2)}) collective-permute-start(f32[4,16,8,128]{3,2,1,0:T(8,128)} %get-tuple-element.26), channel_id=1, source_target_pairs={{0,5},{1,4},{2,7},{3,6},{4,1},{5,0},{6,3},{7,2},{8,13},{9,12},{10,... | collective-permute-start | bytes 786440 | tf_op jit(solution)/shard_map/ppermute | solution.py:320
  13.2 33.5 %collective-permute-start.5 = (f32[4,16,8,128]{3,2,1,0:T(8,128)S(1)}, f32[4,16,8,128]{3,2,1,0:T(8,128)S(1)}, u32[]{:S(2)}, u32[]{:S(2)}) collective-permute-start(f32[4,16,8,128]{3,2,1,0:T(8,128)S(1)} %copy-done.21), channel_id=1, source_target_pairs={{0,6},{1,7},{2,4},{3,5},{4,2},{5,3},{6,0},{7,1},{8,14},{9,15},{10,... | collective-permute-start | bytes 786440 | tf_op jit(solution)/shard_map/ppermute | solution.py:320
  27.1 19.6 %collective-permute-start.6 = (f32[4,16,8,128]{3,2,1,0:T(8,128)S(1)}, f32[4,16,8,128]{3,2,1,0:T(8,128)S(1)}, u32[]{:S(2)}, u32[]{:S(2)}) collective-permute-start(f32[4,16,8,128]{3,2,1,0:T(8,128)S(1)} %copy-done.20), channel_id=1, source_target_pairs={{0,7},{1,6},{2,5},{3,4},{4,3},{5,2},{6,1},{7,0},{8,15},{9,14},{10,... | collective-permute-start | bytes 786440 | tf_op jit(solution)/shard_map/ppermute | solution.py:320
  46.7 335.7 %all-to-all-start = ((f32[32,16,56,128]{3,2,1,0:T(8,128)}), f32[32,16,56,128]{3,2,1,0:T(8,128)}, u32[]{:S(2)}, u32[]{:S(2)}) async-start(f32[32,16,56,128]{3,2,1,0:T(8,128)} %shard_map.120), calls=%async_computation | async-start | bytes 29360128 | tf_op jit(solution)/shard_map/all_to_all | solution.py:373
  67.9 130.4 %collective-permute-start.9 = (f32[8,16,8,128]{3,2,1,0:T(8,128)S(1)}, f32[8,16,8,128]{3,2,1,0:T(8,128)}, u32[]{:S(2)}, u32[]{:S(2)}) collective-permute-start(f32[8,16,8,128]{3,2,1,0:T(8,128)S(1)} %get-tuple-element.87), channel_id=1, source_target_pairs={{0,24},{8,16},{16,8},{24,0},{1,25},{9,17},{17,9},{25,1},{2,26},{10... | collective-permute-start | bytes 1572872 | tf_op jit(solution)/shard_map/ppermute | solution.py:320
  70.5 127.8 %collective-permute-start.8 = (f32[8,16,8,128]{3,2,1,0:T(8,128)S(1)}, f32[8,16,8,128]{3,2,1,0:T(8,128)}, u32[]{:S(2)}, u32[]{:S(2)}) collective-permute-start(f32[8,16,8,128]{3,2,1,0:T(8,128)S(1)} %get-tuple-element.88), channel_id=1, source_target_pairs={{0,16},{8,24},{16,0},{24,8},{1,17},{9,25},{17,1},{25,9},{2,18},{10... | collective-permute-start | bytes 1572872 | tf_op jit(solution)/shard_map/ppermute | solution.py:320
  71.0 139.5 %collective-permute-start.7 = (f32[8,16,8,128]{3,2,1,0:T(8,128)S(1)}, f32[8,16,8,128]{3,2,1,0:T(8,128)}, u32[]{:S(2)}, u32[]{:S(2)}) collective-permute-start(f32[8,16,8,128]{3,2,1,0:T(8,128)S(1)} %get-tuple-element.89), channel_id=1, source_target_pairs={{0,8},{8,0},{16,24},{24,16},{1,9},{9,1},{17,25},{25,17},{2,10},{10... | collective-permute-start | bytes 1572872 | tf_op jit(solution)/shard_map/ppermute | solution.py:320
  382.4 368.6 %all-to-all-start.1 = ((f32[32,16,64,128]{3,2,1,0:T(8,128)}), f32[32,16,64,128]{3,2,1,0:T(8,128)}, u32[]{:S(2)}, u32[]{:S(2)}) async-start(f32[32,16,64,128]{3,2,1,0:T(8,128)} %shard_map.119), calls=%async_computation.1 | async-start | bytes 33554432 | tf_op jit(solution)/shard_map/all_to_all | solution.py:373
  751.0 368.6 %all-to-all-start.2 = ((f32[32,16,64,128]{3,2,1,0:T(8,128)}), f32[32,16,64,128]{3,2,1,0:T(8,128)}, u32[]{:S(2)}, u32[]{:S(2)}) async-start(f32[32,16,64,128]{3,2,1,0:T(8,128)} %shard_map.122), calls=%async_computation.2 | async-start | bytes 33554432 | tf_op jit(solution)/shard_map/all_to_all | solution.py:373
  1119.6 335.0 %all-to-all-start.3 = ((f32[32,16,56,128]{3,2,1,0:T(8,128)}), f32[32,16,56,128]{3,2,1,0:T(8,128)}, u32[]{:S(2)}, u32[]{:S(2)}) async-start(f32[32,16,56,128]{3,2,1,0:T(8,128)} %get-tuple-element.34), calls=%async_computation.3 | async-start | bytes 29360128 | tf_op jit(solution)/shard_map/all_to_all | solution.py:373
  1128.2 119.0 %collective-permute-start.10 = (f32[8,16,8,128]{3,2,1,0:T(8,128)S(1)}, f32[8,16,8,128]{3,2,1,0:T(8,128)S(1)}, u32[]{:S(2)}, u32[]{:S(2)}) collective-permute-start(f32[8,16,8,128]{3,2,1,0:T(8,128)S(1)} %get-tuple-element.45), channel_id=1, source_target_pairs={{0,8},{8,0},{16,24},{24,16},{1,9},{9,1},{17,25},{25,17},{2,10},{10... | collective-permute-start | bytes 1572872 | tf_op jit(solution)/shard_map/ppermute | solution.py:320
  1129.9 138.6 %collective-permute-start.12 = (f32[8,16,8,128]{3,2,1,0:T(8,128)S(1)}, f32[8,16,8,128]{3,2,1,0:T(8,128)S(1)}, u32[]{:S(2)}, u32[]{:S(2)}) collective-permute-start(f32[8,16,8,128]{3,2,1,0:T(8,128)S(1)} %get-tuple-element.46), channel_id=1, source_target_pairs={{0,24},{8,16},{16,8},{24,0},{1,25},{9,17},{17,9},{25,1},{2,26},{10... | collective-permute-start | bytes 1572872 | tf_op jit(solution)/shard_map/ppermute | solution.py:320
  1131.4 137.2 %collective-permute-start.11 = (f32[8,16,8,128]{3,2,1,0:T(8,128)S(1)}, f32[8,16,8,128]{3,2,1,0:T(8,128)S(1)}, u32[]{:S(2)}, u32[]{:S(2)}) collective-permute-start(f32[8,16,8,128]{3,2,1,0:T(8,128)S(1)} %get-tuple-element.47), channel_id=1, source_target_pairs={{0,16},{8,24},{16,0},{24,8},{1,17},{9,25},{17,1},{25,9},{2,18},{10... | collective-permute-start | bytes 1572872 | tf_op jit(solution)/shard_map/ppermute | solution.py:320
  1268.6 186.0 %collective-permute-start.13 = (f32[4,16,8,128]{3,2,1,0:T(8,128)S(1)}, f32[4,16,8,128]{3,2,1,0:T(8,128)S(1)}, u32[]{:S(2)}, u32[]{:S(2)}) collective-permute-start(f32[4,16,8,128]{3,2,1,0:T(8,128)S(1)} %pad_maximum_fusion.8), channel_id=1, source_target_pairs={{0,1},{1,0},{2,3},{3,2},{4,5},{5,4},{6,7},{7,6},{8,9},{9,8},{10,11... | collective-permute-start | bytes 786440 | tf_op jit(solution)/shard_map/ppermute | solution.py:320
  1268.7 185.9 %collective-permute-start.14 = (f32[4,16,8,128]{3,2,1,0:T(8,128)S(1)}, f32[4,16,8,128]{3,2,1,0:T(8,128)S(1)}, u32[]{:S(2)}, u32[]{:S(2)}) collective-permute-start(f32[4,16,8,128]{3,2,1,0:T(8,128)S(1)} %pad_maximum_fusion.9), channel_id=1, source_target_pairs={{0,2},{1,3},{2,0},{3,1},{4,6},{5,7},{6,4},{7,5},{8,10},{9,11},{10,... | collective-permute-start | bytes 786440 | tf_op jit(solution)/shard_map/ppermute | solution.py:320
  1268.9 209.0 %collective-permute-start.15 = (f32[4,16,8,128]{3,2,1,0:T(8,128)S(1)}, f32[4,16,8,128]{3,2,1,0:T(8,128)S(1)}, u32[]{:S(2)}, u32[]{:S(2)}) collective-permute-start(f32[4,16,8,128]{3,2,1,0:T(8,128)S(1)} %pad_maximum_fusion.10), channel_id=1, source_target_pairs={{0,3},{1,2},{2,1},{3,0},{4,7},{5,6},{6,5},{7,4},{8,11},{9,10},{10,... | collective-permute-start | bytes 786440 | tf_op jit(solution)/shard_map/ppermute | solution.py:320
  1270.8 207.1 %collective-permute-start.16 = (f32[4,16,8,128]{3,2,1,0:T(8,128)S(1)}, f32[4,16,8,128]{3,2,1,0:T(8,128)S(1)}, u32[]{:S(2)}, u32[]{:S(2)}) collective-permute-start(f32[4,16,8,128]{3,2,1,0:T(8,128)S(1)} %pad_maximum_fusion.11), channel_id=1, source_target_pairs={{0,4},{1,5},{2,6},{3,7},{4,0},{5,1},{6,2},{7,3},{8,12},{9,13},{10,... | collective-permute-start | bytes 786440 | tf_op jit(solution)/shard_map/ppermute | solution.py:320
  1296.3 181.6 %collective-permute-start.17 = (f32[4,16,8,128]{3,2,1,0:T(8,128)S(1)}, f32[4,16,8,128]{3,2,1,0:T(8,128)S(1)}, u32[]{:S(2)}, u32[]{:S(2)}) collective-permute-start(f32[4,16,8,128]{3,2,1,0:T(8,128)S(1)} %pad_maximum_fusion.12), channel_id=1, source_target_pairs={{0,5},{1,4},{2,7},{3,6},{4,1},{5,0},{6,3},{7,2},{8,13},{9,12},{10,... | collective-permute-start | bytes 786440 | tf_op jit(solution)/shard_map/ppermute | solution.py:320
  1454.6 23.3 %collective-permute-start.18 = (f32[4,16,8,128]{3,2,1,0:T(8,128)S(1)}, f32[4,16,8,128]{3,2,1,0:T(8,128)S(1)}, u32[]{:S(2)}, u32[]{:S(2)}) collective-permute-start(f32[4,16,8,128]{3,2,1,0:T(8,128)S(1)} %pad_maximum_fusion.13), channel_id=1, source_target_pairs={{0,6},{1,7},{2,4},{3,5},{4,2},{5,3},{6,0},{7,1},{8,14},{9,15},{10,... | collective-permute-start | bytes 786440 | tf_op jit(solution)/shard_map/ppermute | solution.py:320
  1454.6 23.3 %collective-permute-start.19 = (f32[4,16,8,128]{3,2,1,0:T(8,128)S(1)}, f32[4,16,8,128]{3,2,1,0:T(8,128)S(1)}, u32[]{:S(2)}, u32[]{:S(2)}) collective-permute-start(f32[4,16,8,128]{3,2,1,0:T(8,128)S(1)} %pad_maximum_fusion.14), channel_id=1, source_target_pairs={{0,7},{1,6},{2,5},{3,4},{4,3},{5,2},{6,1},{7,0},{8,15},{9,14},{10,... | collective-permute-start | bytes 786440 | tf_op jit(solution)/shard_map/ppermute | solution.py:320
  (23 other events, 816.5 us)

commit v4 on v3

--- a/solution.py
+++ b/solution.py
@@ -373,29 +373,28 @@
         return lax.all_to_all(block, BOTH, split_axis=0, concat_axis=0, tiled=True)
 
     end = ROWS if tiled and y_size > ROWS and k_size % ROWS == 0 else 0
-    there, previous = [], None
-    for c in range(count):
-        blocks, first = [], 0
-        if end and c == 0:
-            small = z_in_first(columns, basis_in_z, me, groups, slots)
-            small = swap(small, "pen")
-            previous = small[1:]
-            small = swap(turn(small), "grp")
-            blocks, first = [jnp.concatenate(small)], end
-        table = after(in_table, *small[1:]) if end and c == 1 else in_table
-        out = to_z(columns, c, table, members, first, y_size - first)
+    order = [*range(1, count), 0]
+    there, previous, small = {}, None, None
+    if end:
+        small = swap(z_in_first(columns, basis_in_z, me, groups, slots), "pen")
+        previous = small[1 : slots - slots // LATE]
+    for c in order:
+        first = end if c == 0 else 0
+        out = to_z(columns, c, in_table, members, first, y_size - first)
         out = exchange(after(out, *previous) if previous else out)
         previous = [out]
-        there.append([*blocks, out])
-    back, previous = [], None
-    for c in range(count):
-        cuts = [end, y_size - end] if end and c == count - 1 else [y_size]
+        there[c] = [out]
+    if end:
+        there[0].insert(0, jnp.concatenate(swap(turn(small), "grp")))
+    back, previous = {}, None
+    for c in order:
+        cuts = [end, y_size - end] if end and c == 0 else [y_size]
         outs = across(
             there[c], cuts, [end], me, groups, tables, eig_x, eig_y, levels, shift[c]
         )
         out = exchange(after(outs[-1], *previous) if previous else outs[-1])
         previous = [out]
-        back.append([(y_size - cuts[-1], [out], out_table)])
+        back[c] = [(y_size - cuts[-1], [out], out_table)]
         if len(cuts) > 1:
             small = outs[0].reshape(groups, slots, *outs[0].shape[1:])
             small = turn(swap([small[t] for t in range(groups)], "grp"))
@@ -405,7 +404,7 @@
             )
             back[c].append((0, small, slot_out_table))
     result = None
-    for c in range(count):
+    for c in order:
         for first, blocks, table in back[c]:
             result = from_z(blocks, table, c, columns.shape, result, first)
     return result

time: 1490 us -> 1590 us (1.067)
  starting transfers between devices: 76 us -> 151 us
  waiting for transfers between devices: 1160 us -> 1190 us
    ppermute x20, waiting for transfers between devices: 264 us -> 465 us  [swap(): got[s] = lax.ppermute(blocks[s], axis, [(m, m ^ s) for m in range(size)])]
    all_to_all x4, waiting for transfers between devices: 899 us -> 729 us  [exchange(): return lax.all_to_all(block, BOTH, split_axis=0, concat_axis=0, tiled=True)]
    all_to_all x4, starting transfers between devices: 27.9 us -> 105 us  [exchange(): return lax.all_to_all(block, BOTH, split_axis=0, concat_axis=0, tiled=True)]
  transfers between devices with their start and end apart: 24 -> 24, of which waited for: 9 -> 12; matrix products, arithmetic and copies ran while one was open for 2% -> 1% of each run, Pallas kernels for 14% -> 13%
where the time goes in v4:
time: 1590 us
  waiting for transfers between devices  1190 us (75%)
  Pallas kernels  217 us (14%)
  starting transfers between devices  151 us (9%)
    all_to_all x4, waiting for transfers between devices, exchange(): return lax.all_to_all(block, BOTH, split_axis=0, concat_axis=0, tiled=True)  729 us
    ppermute x20, waiting for transfers between devices, swap(): got[s] = lax.ppermute(blocks[s], axis, [(m, m ^ s) for m in range(size)])  465 us
    pallas_call x2, Pallas kernels, planes(): pl.pallas_call(body, grid=(k_size,), in_specs=[block(b.shape[2]) for b in...  124 us
    all_to_all x4, starting transfers between devices, exchange(): return lax.all_to_all(block, BOTH, split_axis=0, concat_axis=0, tiled=True)  105 us
    pallas_call x3, Pallas kernels, z_out(): pl.pallas_call(body, grid=(y_size // ROWS,), in_specs=[pl.BlockSpec((memb...  48 us
    ppermute x20, starting transfers between devices, swap(): got[s] = lax.ppermute(blocks[s], axis, [(m, m ^ s) for m in range(size)])  46.4 us
    pallas_call x2, Pallas kernels, z_in(): pl.pallas_call(body, grid=(y_size // ROWS,), in_specs=[tile(t) for t in r...  39.9 us
  transfers between devices with their start and end apart: 24, of which 12 were waited for; matrix products, arithmetic and copies ran while one was open for 1% of the time, Pallas kernels for 13%

profile of v4, /device:TPU:0, one launch (start us, length us, event | category | flops | bytes accessed | tf_op | source)
XLA Modules:
  0.0 1586.1 jit_solution(8706541838619934613)
XLA Ops:
  0.7 5.2 shard_map.118
  13.3 21.0 %shard_map.120 = f32[32,16,64,128]{3,2,1,0:T(8,128)} custom-call(f32[2,128,64,512]{3,2,1,0:T(8,128)} %refs_3_.5, f32[2,128,64,512]{3,2,1,0:T(8,128)} %refs_3_.5, f32[2,128,64,512]{3,2,1,0:T(8,128)} %refs_3_.5, f32[2,128,64,512]{3,2,1,0:T(8,128)} %refs_3_.5, bf16[512,1536]{1,0:T(8,128)(2,1)} %pad_maximum_fusion.refs_4_), custom_call_target="tpu_custom_call" | custom-call | flops 12884901888 | bytes 33554432 | tf_op jit(solution)/shard_map/pallas_call | solution.py:79
  35.2 6.1 all-to-all-start
  41.3 18.9 %shard_map.119 = f32[32,16,56,128]{3,2,1,0:T(8,128)} custom-call(f32[2,128,64,512]{3,2,1,0:T(8,128)} %refs_3_.5, f32[2,128,64,512]{3,2,1,0:T(8,128)} %refs_3_.5, f32[2,128,64,512]{3,2,1,0:T(8,128)} %refs_3_.5, f32[2,128,64,512]{3,2,1,0:T(8,128)} %refs_3_.5, bf16[512,1536]{1,0:T(8,128)(2,1)} %pad_maximum_fusion.refs_4_), custom_call_target="tpu_custom_call" | custom-call | flops 11274289152 | bytes 29360128 | tf_op jit(solution)/shard_map/pallas_call | solution.py:79
  60.2 345.7 %all-to-all-done.refs_0_ = f32[32,16,64,128]{3,2,1,0:T(8,128)} async-done(((f32[32,16,64,128]{3,2,1,0:T(8,128)}), f32[32,16,64,128]{3,2,1,0:T(8,128)}, u32[]{:S(2)}, u32[]{:S(2)}) %all-to-all-start) | async-done | bytes 16777248 | tf_op jit(solution)/shard_map/all_to_all | solution.py:373
  405.9 3.8 all-to-all-start.1
  420.1 61.5 %shard_map.122 = f32[32,16,64,128]{3,2,1,0:T(8,128)} custom-call(f32[32,16,64,128]{3,2,1,0:T(8,128)} %all-to-all-done.refs_0_, bf16[512,1536]{1,0:T(8,128)(2,1)} %get-tuple-element.120.refs_2_.refs_1_, bf16[1536,512]{1,0:T(8,128)(2,1)} %get-tuple-element.122.refs_3_.refs_2_, bf16[1536,512]{1,0:T(8,128)(2,1)} %get-tuple-element.123.refs_4_.refs_3_, ...), custom_call_target="tpu_custom_call" | custom-call | flops 51539607552 | bytes 33554432 | tf_op jit(solution)/shard_map/pallas_call | solution.py:200
  481.6 247.9 %all-to-all-done.1.refs_1_ = f32[32,16,56,128]{3,2,1,0:T(8,128)} async-done(((f32[32,16,56,128]{3,2,1,0:T(8,128)}), f32[32,16,56,128]{3,2,1,0:T(8,128)}, u32[]{:S(2)}, u32[]{:S(2)}) %all-to-all-start.1) | async-done | bytes 14680096 | tf_op jit(solution)/shard_map/all_to_all | solution.py:373
  729.5 4.1 all-to-all-start.2
  738.2 276.8 %collective-permute-done.5 = f32[4,16,8,128]{3,2,1,0:T(8,128)S(1)} collective-permute-done((f32[4,16,8,128]{3,2,1,0:T(8,128)}, f32[4,16,8,128]{3,2,1,0:T(8,128)S(1)}, u32[]{:S(2)}, u32[]{:S(2)}) %collective-permute-start.5) | collective-permute-done | bytes 262176 | tf_op jit(solution)/shard_map/ppermute | solution.py:320
  1015.0 4.6 collective-permute-done.6
  1023.2 15.0 collective-permute-done.7
  1038.2 6.8 collective-permute-done.8
  1045.1 11.4 collective-permute-done.9
  1057.8 62.1 %shard_map.121 = (f32[32,16,8,128]{3,2,1,0:T(8,128)}, f32[32,16,56,128]{3,2,1,0:T(8,128)}) custom-call(f32[32,16,8,128]{3,2,1,0:T(8,128)} %copy-done.24, f32[32,16,56,128]{3,2,1,0:T(8,128)} %all-to-all-done.1.refs_1_, bf16[512,1536]{1,0:T(8,128)(2,1)} %get-tuple-element.120.refs_2_.refs_1_, bf16[1536,512]{1,0:T(8,128)(2,1)} %get-tuple-element.122.refs_3_.refs_2_, ...), custom_call_target="tpu_custom_call" | custom-call | flops 51539607552 | bytes 33554432 | tf_op jit(solution)/shard_map/pallas_call | solution.py:200
  1120.0 91.0 %all-to-all-start.3 = ((f32[32,16,56,128]{3,2,1,0:T(8,128)}), f32[32,16,56,128]{3,2,1,0:T(8,128)}, u32[]{:S(2)}, u32[]{:S(2)}) async-start(f32[32,16,56,128]{3,2,1,0:T(8,128)} %get-tuple-element.32), calls=%async_computation.3 | async-start | bytes 29360128 | tf_op jit(solution)/shard_map/all_to_all | solution.py:373
  1220.5 114.2 %collective-permute-done.10 = f32[8,16,8,128]{3,2,1,0:T(8,128)S(1)} collective-permute-done((f32[8,16,8,128]{3,2,1,0:T(8,128)S(1)}, f32[8,16,8,128]{3,2,1,0:T(8,128)S(1)}, u32[]{:S(2)}, u32[]{:S(2)}) %collective-permute-start.10) | collective-permute-done | bytes 524320 | tf_op jit(solution)/shard_map/ppermute | solution.py:320
  1334.9 21.3 %collective-permute-done.12 = f32[8,16,8,128]{3,2,1,0:T(8,128)S(1)} collective-permute-done((f32[8,16,8,128]{3,2,1,0:T(8,128)S(1)}, f32[8,16,8,128]{3,2,1,0:T(8,128)S(1)}, u32[]{:S(2)}, u32[]{:S(2)}) %collective-permute-start.12) | collective-permute-done | bytes 524320 | tf_op jit(solution)/shard_map/ppermute | solution.py:320
  1358.5 24.9 %collective-permute-start.15 = (f32[4,16,8,128]{3,2,1,0:T(8,128)S(1)}, f32[4,16,8,128]{3,2,1,0:T(8,128)S(1)}, u32[]{:S(2)}, u32[]{:S(2)}) collective-permute-start(f32[4,16,8,128]{3,2,1,0:T(8,128)S(1)} %pad_maximum_fusion.10), channel_id=1, source_target_pairs={{0,3},{1,2},{2,1},{3,0},{4,7},{5,6},{6,5},{7,4},{8,11},{9,10},{10,... | collective-permute-start | bytes 786440 | tf_op jit(solution)/shard_map/ppermute | solution.py:320
  1384.7 22.3 %shard_map.123.refs_2_ = f32[2,128,64,512]{3,2,1,0:T(8,128)} custom-call(f32[32,16,64,128]{3,2,1,0:T(8,128)} %all-to-all-done.2.refs_0_, bf16[1536,512]{1,0:T(8,128)(2,1)} %pad_maximum_fusion.6.refs_1_), custom_call_target="tpu_custom_call" | custom-call | flops 12884901888 | bytes 33554432 | tf_op jit(solution)/shard_map/pallas_call | solution.py:252
  1407.0 135.0 %all-to-all-done.3.refs_0_ = f32[32,16,56,128]{3,2,1,0:T(8,128)} async-done(((f32[32,16,56,128]{3,2,1,0:T(8,128)}), f32[32,16,56,128]{3,2,1,0:T(8,128)}, u32[]{:S(2)}, u32[]{:S(2)}) %all-to-all-start.3) | async-done | bytes 14680096 | tf_op jit(solution)/shard_map/all_to_all | solution.py:373
  1547.1 10.8 collective-permute-done.16.refs_4_
  1558.7 20.0 %shard_map.124.refs_9_ = f32[2,128,64,512]{3,2,1,0:T(8,128)} custom-call(f32[32,16,56,128]{3,2,1,0:T(8,128)} %all-to-all-done.3.refs_0_, bf16[1536,512]{1,0:T(8,128)(2,1)} %pad_maximum_fusion.6.refs_1_, f32[2,128,64,512]{3,2,1,0:T(8,128)} %shard_map.123.refs_2_), custom_call_target="tpu_custom_call", output_to_operand_aliasing={{}: (2, {})} | custom-call | flops 11274289152 | bytes 29360128 | tf_op jit(solution)/shard_map/pallas_call | solution.py:252
  1580.4 5.7 shard_map.125
  (135 shorter events, 49.5 us)
Async XLA Ops:
  5.9 28.4 %collective-permute-start = (f32[4,16,8,128]{3,2,1,0:T(8,128)}, f32[4,16,8,128]{3,2,1,0:T(8,128)S(1)}, u32[]{:S(2)}, u32[]{:S(2)}) collective-permute-start(f32[4,16,8,128]{3,2,1,0:T(8,128)} %get-tuple-element.21), channel_id=1, source_target_pairs={{0,1},{1,0},{2,3},{3,2},{4,5},{5,4},{6,7},{7,6},{8,9},{9,8},{10,11... | collective-permute-start | bytes 786440 | tf_op jit(solution)/shard_map/ppermute | solution.py:320
  6.4 27.9 %collective-permute-start.1 = (f32[4,16,8,128]{3,2,1,0:T(8,128)}, f32[4,16,8,128]{3,2,1,0:T(8,128)S(1)}, u32[]{:S(2)}, u32[]{:S(2)}) collective-permute-start(f32[4,16,8,128]{3,2,1,0:T(8,128)} %get-tuple-element.22), channel_id=1, source_target_pairs={{0,2},{1,3},{2,0},{3,1},{4,6},{5,7},{6,4},{7,5},{8,10},{9,11},{10,... | collective-permute-start | bytes 786440 | tf_op jit(solution)/shard_map/ppermute | solution.py:320
  9.0 25.3 %collective-permute-start.2 = (f32[4,16,8,128]{3,2,1,0:T(8,128)}, f32[4,16,8,128]{3,2,1,0:T(8,128)S(1)}, u32[]{:S(2)}, u32[]{:S(2)}) collective-permute-start(f32[4,16,8,128]{3,2,1,0:T(8,128)} %get-tuple-element.23), channel_id=1, source_target_pairs={{0,3},{1,2},{2,1},{3,0},{4,7},{5,6},{6,5},{7,4},{8,11},{9,10},{10,... | collective-permute-start | bytes 786440 | tf_op jit(solution)/shard_map/ppermute | solution.py:320
  9.1 26.0 %collective-permute-start.3 = (f32[4,16,8,128]{3,2,1,0:T(8,128)}, f32[4,16,8,128]{3,2,1,0:T(8,128)}, u32[]{:S(2)}, u32[]{:S(2)}) collective-permute-start(f32[4,16,8,128]{3,2,1,0:T(8,128)} %get-tuple-element.24), channel_id=1, source_target_pairs={{0,4},{1,5},{2,6},{3,7},{4,0},{5,1},{6,2},{7,3},{8,12},{9,13},{10,... | collective-permute-start | bytes 786440 | tf_op jit(solution)/shard_map/ppermute | solution.py:320
  11.8 23.4 %collective-permute-start.4 = (f32[4,16,8,128]{3,2,1,0:T(8,128)}, f32[4,16,8,128]{3,2,1,0:T(8,128)S(1)}, u32[]{:S(2)}, u32[]{:S(2)}) collective-permute-start(f32[4,16,8,128]{3,2,1,0:T(8,128)} %get-tuple-element.25), channel_id=1, source_target_pairs={{0,5},{1,4},{2,7},{3,6},{4,1},{5,0},{6,3},{7,2},{8,13},{9,12},{10,... | collective-permute-start | bytes 786440 | tf_op jit(solution)/shard_map/ppermute | solution.py:320
  35.2 370.7 %all-to-all-start = ((f32[32,16,64,128]{3,2,1,0:T(8,128)}), f32[32,16,64,128]{3,2,1,0:T(8,128)}, u32[]{:S(2)}, u32[]{:S(2)}) async-start(f32[32,16,64,128]{3,2,1,0:T(8,128)} %shard_map.120), calls=%async_computation | async-start | bytes 33554432 | tf_op jit(solution)/shard_map/all_to_all | solution.py:373
  405.9 323.6 %all-to-all-start.1 = ((f32[32,16,56,128]{3,2,1,0:T(8,128)}), f32[32,16,56,128]{3,2,1,0:T(8,128)}, u32[]{:S(2)}, u32[]{:S(2)}) async-start(f32[32,16,56,128]{3,2,1,0:T(8,128)} %shard_map.119), calls=%async_computation.1 | async-start | bytes 29360128 | tf_op jit(solution)/shard_map/all_to_all | solution.py:373
  729.5 390.4 %all-to-all-start.2 = ((f32[32,16,64,128]{3,2,1,0:T(8,128)}), f32[32,16,64,128]{3,2,1,0:T(8,128)}, u32[]{:S(2)}, u32[]{:S(2)}) async-start(f32[32,16,64,128]{3,2,1,0:T(8,128)} %shard_map.122), calls=%async_computation.2 | async-start | bytes 33554432 | tf_op jit(solution)/shard_map/all_to_all | solution.py:373
  733.6 281.4 %collective-permute-start.5 = (f32[4,16,8,128]{3,2,1,0:T(8,128)}, f32[4,16,8,128]{3,2,1,0:T(8,128)S(1)}, u32[]{:S(2)}, u32[]{:S(2)}) collective-permute-start(f32[4,16,8,128]{3,2,1,0:T(8,128)} %get-tuple-element.26), channel_id=1, source_target_pairs={{0,6},{1,7},{2,4},{3,5},{4,2},{5,3},{6,0},{7,1},{8,14},{9,15},{10,... | collective-permute-start | bytes 786440 | tf_op jit(solution)/shard_map/ppermute | solution.py:320
  737.1 282.6 %collective-permute-start.6 = (f32[4,16,8,128]{3,2,1,0:T(8,128)}, f32[4,16,8,128]{3,2,1,0:T(8,128)S(1)}, u32[]{:S(2)}, u32[]{:S(2)}) collective-permute-start(f32[4,16,8,128]{3,2,1,0:T(8,128)} %get-tuple-element.27), channel_id=1, source_target_pairs={{0,7},{1,6},{2,5},{3,4},{4,3},{5,2},{6,1},{7,0},{8,15},{9,14},{10,... | collective-permute-start | bytes 786440 | tf_op jit(solution)/shard_map/ppermute | solution.py:320
  1019.7 18.5 %collective-permute-start.7 = (f32[8,16,8,128]{3,2,1,0:T(8,128)S(1)}, f32[8,16,8,128]{3,2,1,0:T(8,128)S(1)}, u32[]{:S(2)}, u32[]{:S(2)}) collective-permute-start(f32[8,16,8,128]{3,2,1,0:T(8,128)S(1)} %get-tuple-element.86), channel_id=1, source_target_pairs={{0,8},{8,0},{16,24},{24,16},{1,9},{9,1},{17,25},{25,17},{2,10},{10... | collective-permute-start | bytes 1572872 | tf_op jit(solution)/shard_map/ppermute | solution.py:320
  1021.4 23.7 %collective-permute-start.8 = (f32[8,16,8,128]{3,2,1,0:T(8,128)S(1)}, f32[8,16,8,128]{3,2,1,0:T(8,128)S(1)}, u32[]{:S(2)}, u32[]{:S(2)}) collective-permute-start(f32[8,16,8,128]{3,2,1,0:T(8,128)S(1)} %get-tuple-element.85), channel_id=1, source_target_pairs={{0,16},{8,24},{16,0},{24,8},{1,17},{9,25},{17,1},{25,9},{2,18},{10... | collective-permute-start | bytes 1572872 | tf_op jit(solution)/shard_map/ppermute | solution.py:320
  1022.7 33.8 %collective-permute-start.9 = (f32[8,16,8,128]{3,2,1,0:T(8,128)S(1)}, f32[8,16,8,128]{3,2,1,0:T(8,128)S(1)}, u32[]{:S(2)}, u32[]{:S(2)}) collective-permute-start(f32[8,16,8,128]{3,2,1,0:T(8,128)S(1)} %get-tuple-element.84), channel_id=1, source_target_pairs={{0,24},{8,16},{16,8},{24,0},{1,25},{9,17},{17,9},{25,1},{2,26},{10... | collective-permute-start | bytes 1572872 | tf_op jit(solution)/shard_map/ppermute | solution.py:320
  1120.0 422.0 %all-to-all-start.3 = ((f32[32,16,56,128]{3,2,1,0:T(8,128)}), f32[32,16,56,128]{3,2,1,0:T(8,128)}, u32[]{:S(2)}, u32[]{:S(2)}) async-start(f32[32,16,56,128]{3,2,1,0:T(8,128)} %get-tuple-element.32), calls=%async_computation.3 | async-start | bytes 29360128 | tf_op jit(solution)/shard_map/all_to_all | solution.py:373
  1214.4 120.4 %collective-permute-start.10 = (f32[8,16,8,128]{3,2,1,0:T(8,128)S(1)}, f32[8,16,8,128]{3,2,1,0:T(8,128)S(1)}, u32[]{:S(2)}, u32[]{:S(2)}) collective-permute-start(f32[8,16,8,128]{3,2,1,0:T(8,128)S(1)} %get-tuple-element.43), channel_id=1, source_target_pairs={{0,8},{8,0},{16,24},{24,16},{1,9},{9,1},{17,25},{25,17},{2,10},{10... | collective-permute-start | bytes 1572872 | tf_op jit(solution)/shard_map/ppermute | solution.py:320
  1217.4 117.4 %collective-permute-start.11 = (f32[8,16,8,128]{3,2,1,0:T(8,128)S(1)}, f32[8,16,8,128]{3,2,1,0:T(8,128)S(1)}, u32[]{:S(2)}, u32[]{:S(2)}) collective-permute-start(f32[8,16,8,128]{3,2,1,0:T(8,128)S(1)} %get-tuple-element.45), channel_id=1, source_target_pairs={{0,16},{8,24},{16,0},{24,8},{1,17},{9,25},{17,1},{25,9},{2,18},{10... | collective-permute-start | bytes 1572872 | tf_op jit(solution)/shard_map/ppermute | solution.py:320
  1220.2 135.9 %collective-permute-start.12 = (f32[8,16,8,128]{3,2,1,0:T(8,128)S(1)}, f32[8,16,8,128]{3,2,1,0:T(8,128)S(1)}, u32[]{:S(2)}, u32[]{:S(2)}) collective-permute-start(f32[8,16,8,128]{3,2,1,0:T(8,128)S(1)} %get-tuple-element.44), channel_id=1, source_target_pairs={{0,24},{8,16},{16,8},{24,0},{1,25},{9,17},{17,9},{25,1},{2,26},{10... | collective-permute-start | bytes 1572872 | tf_op jit(solution)/shard_map/ppermute | solution.py:320
  1356.2 189.5 %collective-permute-start.17 = (f32[4,16,8,128]{3,2,1,0:T(8,128)S(1)}, f32[4,16,8,128]{3,2,1,0:T(8,128)S(1)}, u32[]{:S(2)}, u32[]{:S(2)}) collective-permute-start(f32[4,16,8,128]{3,2,1,0:T(8,128)S(1)} %pad_maximum_fusion.12), channel_id=1, source_target_pairs={{0,5},{1,4},{2,7},{3,6},{4,1},{5,0},{6,3},{7,2},{8,13},{9,12},{10,... | collective-permute-start | bytes 786440 | tf_op jit(solution)/shard_map/ppermute | solution.py:320
  1356.3 201.5 %collective-permute-start.16 = (f32[4,16,8,128]{3,2,1,0:T(8,128)S(1)}, f32[4,16,8,128]{3,2,1,0:T(8,128)S(1)}, u32[]{:S(2)}, u32[]{:S(2)}) collective-permute-start(f32[4,16,8,128]{3,2,1,0:T(8,128)S(1)} %pad_maximum_fusion.11), channel_id=1, source_target_pairs={{0,4},{1,5},{2,6},{3,7},{4,0},{5,1},{6,2},{7,3},{8,12},{9,13},{10,... | collective-permute-start | bytes 786440 | tf_op jit(solution)/shard_map/ppermute | solution.py:320
  1358.5 220.2 %collective-permute-start.15 = (f32[4,16,8,128]{3,2,1,0:T(8,128)S(1)}, f32[4,16,8,128]{3,2,1,0:T(8,128)S(1)}, u32[]{:S(2)}, u32[]{:S(2)}) collective-permute-start(f32[4,16,8,128]{3,2,1,0:T(8,128)S(1)} %pad_maximum_fusion.10), channel_id=1, source_target_pairs={{0,3},{1,2},{2,1},{3,0},{4,7},{5,6},{6,5},{7,4},{8,11},{9,10},{10,... | collective-permute-start | bytes 786440 | tf_op jit(solution)/shard_map/ppermute | solution.py:320
  1383.4 195.3 %collective-permute-start.14 = (f32[4,16,8,128]{3,2,1,0:T(8,128)S(1)}, f32[4,16,8,128]{3,2,1,0:T(8,128)S(1)}, u32[]{:S(2)}, u32[]{:S(2)}) collective-permute-start(f32[4,16,8,128]{3,2,1,0:T(8,128)S(1)} %pad_maximum_fusion.9), channel_id=1, source_target_pairs={{0,2},{1,3},{2,0},{3,1},{4,6},{5,7},{6,4},{7,5},{8,10},{9,11},{10,... | collective-permute-start | bytes 786440 | tf_op jit(solution)/shard_map/ppermute | solution.py:320
  1383.8 195.0 %collective-permute-start.13 = (f32[4,16,8,128]{3,2,1,0:T(8,128)S(1)}, f32[4,16,8,128]{3,2,1,0:T(8,128)S(1)}, u32[]{:S(2)}, u32[]{:S(2)}) collective-permute-start(f32[4,16,8,128]{3,2,1,0:T(8,128)S(1)} %pad_maximum_fusion.8), channel_id=1, source_target_pairs={{0,1},{1,0},{2,3},{3,2},{4,5},{5,4},{6,7},{7,6},{8,9},{9,8},{10,11... | collective-permute-start | bytes 786440 | tf_op jit(solution)/shard_map/ppermute | solution.py:320
  1545.7 33.1 %collective-permute-start.19 = (f32[4,16,8,128]{3,2,1,0:T(8,128)S(1)}, f32[4,16,8,128]{3,2,1,0:T(8,128)S(1)}, u32[]{:S(2)}, u32[]{:S(2)}) collective-permute-start(f32[4,16,8,128]{3,2,1,0:T(8,128)S(1)} %pad_maximum_fusion.14), channel_id=1, source_target_pairs={{0,7},{1,6},{2,5},{3,4},{4,3},{5,2},{6,1},{7,0},{8,15},{9,14},{10,... | collective-permute-start | bytes 786440 | tf_op jit(solution)/shard_map/ppermute | solution.py:320
  1557.8 20.9 %collective-permute-start.18 = (f32[4,16,8,128]{3,2,1,0:T(8,128)S(1)}, f32[4,16,8,128]{3,2,1,0:T(8,128)S(1)}, u32[]{:S(2)}, u32[]{:S(2)}) collective-permute-start(f32[4,16,8,128]{3,2,1,0:T(8,128)S(1)} %pad_maximum_fusion.13), channel_id=1, source_target_pairs={{0,6},{1,7},{2,4},{3,5},{4,2},{5,3},{6,0},{7,1},{8,14},{9,15},{10,... | collective-permute-start | bytes 786440 | tf_op jit(solution)/shard_map/ppermute | solution.py:320
  (26 other events, 1965.6 us)
